TPU v7x, 512 devices: a whole 4x8x8 slice. The times are simulated.
512 devices in a mesh: dp: 8 (over z), expert: 64 (over x, y, core).
Axes of the slice: x: 4, y: 8, z: 8, core: 2. Of those that a mesh axis runs over, the one named last changes fastest.
Arguments:
- tokens: bfloat16 [2048, 2048], P('expert', 'dp'), may hold values from -6 to 6
- cotangent: bfloat16 [2048, 2048], P('expert', 'dp'), may hold values from -6 to 6
- routes: int32 [2048, 8], P('expert'), may hold values from 0 to 63, all different within a row; in each aligned block of 32 rows (0 to 31, 32 to 63, ...) at most 5 rows name the same one
- probs: float32 [2048, 8], P('expert'), may hold values from 0.03 to 0.6
- matching: int32 [64], replicated, may hold values from 0 to 63, as said below
- gate_weight: bfloat16 [64, 2048, 1024], P('expert', None, 'dp'), may hold values from -0.125 to 0.125
- up_weight: bfloat16 [64, 2048, 1024], P('expert', None, 'dp'), may hold values from -0.125 to 0.125
- down_weight: bfloat16 [64, 2048, 1024], P('expert', None, 'dp'), may hold values from -0.1875 to 0.1875
Outputs:
- input_grad: bfloat16 [2048, 2048], P('expert', 'dp')
- gate_weight_grad: float32 [64, 2048, 1024], P('expert', None, 'dp')
- up_weight_grad: float32 [64, 2048, 1024], P('expert', None, 'dp')
- down_weight_grad: float32 [64, 2048, 1024], P('expert', None, 'dp')
Inputs may be any that keep to these rules, and one draw needn't show every extreme that they name: matching pairs the experts: matching[matching[i]] == i and matching[i] != i. `routes`: each token names 8 different experts; within each aligned block of 32 tokens no expert is named by more than 5 tokens.
All inputs are finite; a program needn't handle non-finite values.
Results may differ from a plain program's by a relative error of at most 0.015.
Values may be sent and summed in bfloat16 or wider, within the bound.
No kernel may reach another device: no remote copies, remote signals or barrier semaphores. Data moves between devices by JAX's collectives and lax.ppermute only.
A program may use at most 64 MiB of HBM per device.

v0:
```python
import jax
import jax.numpy as jnp
from jax import lax
from jax.sharding import PartitionSpec as P

contract_rows = (((0,), (0,)), ((), ()))
contract_cols = (((1,), (1,)), ((), ()))


def relay_weights(first, second, third):
    return (
        lax.all_to_all(first, "expert", split_axis=1, concat_axis=0, tiled=True),
        lax.all_to_all(second, "expert", split_axis=1, concat_axis=0, tiled=True),
        lax.all_to_all(third, "expert", split_axis=1, concat_axis=0, tiled=True),
    )


def migrate(arrays, matching, mover):
    experts = matching.shape[0]
    model_width = arrays[0].shape[-2]
    hidden_width = arrays[0].shape[-1]
    piece_rows = model_width // experts
    split = [a.reshape(1, experts, piece_rows, hidden_width) for a in arrays]
    spread = mover(split[0], split[1], split[2])
    ordered = [
        jnp.take(s, matching, axis=0).reshape(1, experts, piece_rows, hidden_width) for s in spread
    ]
    landed = mover(ordered[0], ordered[1], ordered[2])
    return [w.reshape(model_width, hidden_width) for w in landed]


def layout(routes, probs, target_table, capacity):
    experts = target_table.shape[0]
    tok_rows = routes.shape[0]
    top_count = routes.shape[1]
    pair_count = tok_rows * top_count
    pair_expert = routes.reshape(pair_count)
    onehot = (pair_expert[:, None] == jnp.arange(experts, dtype=jnp.int32)[None, :]).astype(
        jnp.int32
    )
    running = jnp.cumsum(onehot, axis=0)
    rank = jnp.sum(onehot * running, axis=1) - 1
    target = jnp.sum(onehot * target_table[None, :], axis=1)
    slot = target * capacity + rank
    slot_total = experts * capacity
    owners = jnp.arange(pair_count, dtype=jnp.int32) // top_count
    slot_token = jnp.full((slot_total,), tok_rows, jnp.int32).at[slot].set(owners)
    slot_prob = jnp.zeros((slot_total,), jnp.float32).at[slot].set(probs.reshape(pair_count))
    return (slot, slot_token, slot_prob)


def build_rows(tokens, cotangent, slot_token, slot_prob):
    blank = jnp.zeros((1, tokens.shape[1]), jnp.bfloat16)
    inputs = jnp.take(jnp.concatenate([tokens, blank], axis=0), slot_token, axis=0)
    picked = jnp.take(jnp.concatenate([cotangent, blank], axis=0), slot_token, axis=0)
    grads = (picked.astype(jnp.float32) * slot_prob[:, None]).astype(jnp.bfloat16)
    return (inputs, grads)


def combine_pairs(returned, slot, tok_rows, top_count):
    rows = jnp.take(returned, slot, axis=0)
    return jnp.sum(rows.reshape(tok_rows, top_count, returned.shape[1]), axis=1)


def expert_grads(inputs, grads, w_gate, w_up, w_down):
    gate = jnp.dot(inputs, w_gate, preferred_element_type=jnp.float32)
    upper = jnp.dot(inputs, w_up, preferred_element_type=jnp.float32)
    sig = jax.nn.sigmoid(gate)
    hidden = (gate * sig * upper).astype(jnp.bfloat16)
    hidden_back = jnp.dot(grads, w_down, preferred_element_type=jnp.float32)
    up_back = (hidden_back * gate * sig).astype(jnp.bfloat16)
    gate_back = (hidden_back * upper * sig * (1.0 + gate * (1.0 - sig))).astype(jnp.bfloat16)
    gate_sum = lax.dot_general(inputs, gate_back, contract_rows, preferred_element_type=jnp.float32)
    up_sum = lax.dot_general(inputs, up_back, contract_rows, preferred_element_type=jnp.float32)
    down_sum = lax.dot_general(grads, hidden, contract_rows, preferred_element_type=jnp.float32)
    return (gate_sum, up_sum, down_sum, gate_back, up_back)


def slice_back(gate_back, up_back, w_gate, w_up):
    first = lax.dot_general(gate_back, w_gate, contract_cols, preferred_element_type=jnp.float32)
    return first + lax.dot_general(up_back, w_up, contract_cols, preferred_element_type=jnp.float32)


def local(tokens, cotangent, routes, probs, matching, gate_weight, up_weight, down_weight):
    experts = matching.shape[0]
    tok_rows = routes.shape[0]
    top_count = routes.shape[1]
    capacity = max(2, 5 * tok_rows * top_count // (4 * experts))
    model_width = gate_weight.shape[1]
    hidden_width = gate_weight.shape[2]
    w_gate, w_up, w_down = migrate((gate_weight, up_weight, down_weight), matching, relay_weights)
    slot, slot_token, slot_prob = layout(routes, probs, matching, capacity)
    whole_in, whole_out = (
        lax.all_gather(tokens, "dp", axis=1, tiled=True),
        lax.all_gather(cotangent, "dp", axis=1, tiled=True),
    )
    inputs, grads = build_rows(whole_in, whole_out, slot_token, slot_prob)
    arrived_in, arrived_out = (
        lax.all_to_all(inputs, "expert", split_axis=0, concat_axis=0, tiled=True),
        lax.all_to_all(grads, "expert", split_axis=0, concat_axis=0, tiled=True),
    )
    gate_sum, up_sum, down_sum, gate_back, up_back = expert_grads(
        arrived_in, arrived_out, w_gate, w_up, w_down
    )
    partial_value = slice_back(gate_back, up_back, w_gate, w_up).astype(jnp.bfloat16)
    pair_back = lax.psum_scatter(partial_value, "dp", scatter_dimension=1, tiled=True).astype(
        jnp.float32
    )
    returned = lax.all_to_all(
        pair_back.astype(jnp.bfloat16), "expert", split_axis=0, concat_axis=0, tiled=True
    ).astype(pair_back.dtype)
    token_sum = combine_pairs(returned, slot, tok_rows, top_count)
    return (
        token_sum.astype(jnp.bfloat16),
        gate_sum.reshape(1, model_width, hidden_width),
        up_sum.reshape(1, model_width, hidden_width),
        down_sum.reshape(1, model_width, hidden_width),
    )


def solution(mesh):
    placed = (
        P("expert", "dp"),
        P("expert", "dp"),
        P("expert", None),
        P("expert", None),
        P(),
        P("expert", None, "dp"),
        P("expert", None, "dp"),
        P("expert", None, "dp"),
    )
    return jax.shard_map(
        local,
        mesh=mesh,
        in_specs=placed,
        out_specs=(
            P("expert", "dp"),
            P("expert", None, "dp"),
            P("expert", None, "dp"),
            P("expert", None, "dp"),
        ),
        check_vma=False,
    )
```

profile of v0, /device:TPU:1, one launch (start us, length us, event | category | flops | bytes accessed | tf_op | source)
XLA Modules:
  0.0 365.8 jit_solution(9097960822106262097)
XLA Ops:
  7.2 29.1 %all_to_all.96 = bf16[1,64,32,128]{3,2,0,1:T(8,128)(2,1)S(1)} all-to-all(bf16[1,64,32,128]{3,2,0,1:T(8,128)(2,1)} %bitcast.85), channel_id=1, replica_groups=mesh['dp'=8,'expert'=64] {'expert'}, dimensions={1} | all-to-all | bytes 1048576 | tf_op jit(solution)/shard_map/all_to_all | solution.py:13
  36.3 23.5 %all_to_all.97 = bf16[1,64,32,128]{3,2,0,1:T(8,128)(2,1)S(1)} all-to-all(bf16[1,64,32,128]{3,2,0,1:T(8,128)(2,1)S(1)} %bitcast.86), channel_id=1, replica_groups=mesh['dp'=8,'expert'=64] {'expert'}, dimensions={1} | all-to-all | bytes 1048576 | tf_op jit(solution)/shard_map/all_to_all | solution.py:12
  59.8 6.3 %all-to-all-start.1 = ((bf16[1,64,32,128]{3,2,0,1:T(8,128)(2,1)}), bf16[1,64,32,128]{3,2,0,1:T(8,128)(2,1)S(1)}, u32[]{:S(2)}, u32[]{:S(2)}) async-start(bf16[1,64,32,128]{3,2,0,1:T(8,128)(2,1)} %bitcast.3), calls=%async_computation.1 | async-start | bytes 1048576 | tf_op jit(solution)/shard_map/all_to_all | solution.py:14
  66.4 0.7 gather_fusion.4
  67.1 0.7 gather_fusion.5
  67.7 15.7 %all-to-all-done.1 = bf16[1,64,32,128]{3,2,0,1:T(8,128)(2,1)S(1)} async-done(((bf16[1,64,32,128]{3,2,0,1:T(8,128)(2,1)}), bf16[1,64,32,128]{3,2,0,1:T(8,128)(2,1)S(1)}, u32[]{:S(2)}, u32[]{:S(2)}) %all-to-all-start.1) | async-done | bytes 524320 | tf_op jit(solution)/shard_map/all_to_all | solution.py:14
  83.4 0.7 gather_fusion.2
  84.1 1.4 fusion.2
  85.4 6.4 %all-to-all-start.7 = ((bf16[1,64,32,128]{3,2,0,1:T(8,128)(2,1)}), bf16[1,64,32,128]{3,2,0,1:T(8,128)(2,1)S(1)}, u32[]{:S(2)}, u32[]{:S(2)}) async-start(bf16[1,64,32,128]{3,2,0,1:T(8,128)(2,1)} %get-tuple-element.11), calls=%async_computation.7 | async-start | bytes 1048576 | tf_op jit(solution)/shard_map/all_to_all | solution.py:12
  91.8 0.6 reduce-window.6
  92.7 26.1 %all_gather.7 = bf16[32,2048]{1,0:T(8,128)(2,1)S(1)} all-gather(bf16[32,256]{1,0:T(8,128)(2,1)S(1)} %copy-done.8), channel_id=1, replica_groups=mesh['dp'=8,'expert'=64] {'dp'}, dimensions={1}, use_global_device_ids=true | all-gather | bytes 147456 | tf_op jit(solution)/shard_map/all_gather | solution.py:94
  118.9 0.6 copy-done.10
  119.5 1.4 scatter_custom_fusion
  120.9 15.2 %all-to-all-start.5 = ((bf16[1,64,32,128]{3,2,0,1:T(8,128)(2,1)}), bf16[1,64,32,128]{3,2,0,1:T(8,128)(2,1)S(1)}, u32[]{:S(2)}, u32[]{:S(2)}) async-start(bf16[1,64,32,128]{3,2,0,1:T(8,128)(2,1)} %get-tuple-element.10), calls=%async_computation.5 | async-start | bytes 1048576 | tf_op jit(solution)/shard_map/all_to_all | solution.py:13
  136.1 2.4 gather_fusion.3
  138.6 0.2 broadcast_select_fusion
  138.8 1.6 all_to_all.76
  140.4 13.0 %all-to-all-done.5 = bf16[1,64,32,128]{3,2,0,1:T(8,128)(2,1)S(1)} async-done(((bf16[1,64,32,128]{3,2,0,1:T(8,128)(2,1)}), bf16[1,64,32,128]{3,2,0,1:T(8,128)(2,1)S(1)}, u32[]{:S(2)}, u32[]{:S(2)}) %all-to-all-start.5) | async-done | bytes 524320 | tf_op jit(solution)/shard_map/all_to_all | solution.py:13
  153.4 0.8 copy-done.2
  154.2 6.3 %all-to-all-start.3 = ((bf16[64,5,2048]{2,1,0:T(8,128)(2,1)}), bf16[64,5,2048]{2,1,0:T(8,128)(2,1)S(1)}, u32[]{:S(2)}, u32[]{:S(2)}) async-start(bf16[64,5,2048]{2,1,0:T(8,128)(2,1)} %all_to_all.76), calls=%async_computation.3 | async-start | bytes 4194304 | tf_op jit(solution)/shard_map/all_to_all | solution.py:99
  160.5 20.2 %all_gather.6 = bf16[32,2048]{1,0:T(8,128)(2,1)S(1)} all-gather(bf16[32,256]{1,0:T(8,128)(2,1)S(1)} %copy-done.9), channel_id=1, replica_groups=mesh['dp'=8,'expert'=64] {'dp'}, dimensions={1}, use_global_device_ids=true | all-gather | bytes 147456 | tf_op jit(solution)/shard_map/all_gather | solution.py:95
  180.8 3.0 gather_fusion.1
  184.0 1.6 scatter_custom_fusion.1
  185.6 1.7 multiply_convert_fusion
  187.3 1.6 all_to_all.70
  188.9 22.9 %all-to-all-done.3 = bf16[64,5,2048]{2,1,0:T(8,128)(2,1)S(1)} async-done(((bf16[64,5,2048]{2,1,0:T(8,128)(2,1)}), bf16[64,5,2048]{2,1,0:T(8,128)(2,1)S(1)}, u32[]{:S(2)}, u32[]{:S(2)}) %all-to-all-start.3) | async-done | bytes 1310752 | tf_op jit(solution)/shard_map/all_to_all | solution.py:99
  211.8 57.2 %all_to_all.98 = bf16[64,5,2048]{2,1,0:T(8,128)(2,1)} all-to-all(bf16[64,5,2048]{2,1,0:T(8,128)(2,1)} %all_to_all.70), channel_id=1, replica_groups=mesh['dp'=8,'expert'=64] {'expert'}, dimensions={0} | all-to-all | bytes 2621440 | tf_op jit(solution)/shard_map/all_to_all | solution.py:100
  268.9 6.0 %all-to-all-start.2 = ((bf16[1,64,32,128]{3,2,0,1:T(8,128)(2,1)}), bf16[1,64,32,128]{3,2,0,1:T(8,128)(2,1)}, u32[]{:S(2)}, u32[]{:S(2)}) async-start(bf16[1,64,32,128]{3,2,0,1:T(8,128)(2,1)} %get-tuple-element.12), calls=%async_computation.2 | async-start | bytes 1048576 | tf_op jit(solution)/shard_map/all_to_all | solution.py:14
  275.0 0.6 all_to_all.78
  275.6 2.6 all_to_all.72
  278.2 0.5 fusion.15
  278.7 0.5 copy-done.3
  279.3 0.5 fusion.14
  279.8 12.4 %all-to-all-done.2 = bf16[1,64,32,128]{3,2,0,1:T(8,128)(2,1)} async-done(((bf16[1,64,32,128]{3,2,0,1:T(8,128)(2,1)}), bf16[1,64,32,128]{3,2,0,1:T(8,128)(2,1)}, u32[]{:S(2)}, u32[]{:S(2)}) %all-to-all-start.2) | async-done | bytes 524320 | tf_op jit(solution)/shard_map/all_to_all | solution.py:14
  292.2 1.5 multiply_convert_fusion.2
  293.8 0.5 fusion.16
  294.4 0.4 copy-done.4
  294.8 1.6 fusion
  296.4 0.6 copy-done.11
  297.2 1.6 convolution_bitcast_fusion.2
  298.8 30.0 %reduce-scatter.2.cloned.1.call-done = bf16[320,256]{1,0:T(8,128)(2,1)} async-done(((bf16[320,2048]{1,0:T(8,128)(2,1)}), bf16[320,256]{1,0:T(8,128)(2,1)}) %reduce-scatter.2.cloned.1.call-update) | async-done | bytes 163856 | tf_op jit(solution)/shard_map/reduce_scatter | solution.py:106
  328.8 1.7 all_to_all.85
  330.5 14.7 %all-to-all-start.8 = ((bf16[64,5,256]{2,1,0:T(8,128)(2,1)}), bf16[64,5,256]{2,1,0:T(8,128)(2,1)S(1)}, u32[]{:S(2)}, u32[]{:S(2)}) async-start(bf16[64,5,256]{2,1,0:T(8,128)(2,1)} %all_to_all.85), calls=%async_computation.9 | async-start | bytes 524288 | tf_op jit(solution)/shard_map/all_to_all | solution.py:109
  345.2 1.6 convolution_bitcast_fusion.1
  346.8 1.6 convolution_bitcast_fusion
  348.4 8.8 %all-to-all-done.8 = bf16[64,5,256]{2,1,0:T(8,128)(2,1)S(1)} async-done(((bf16[64,5,256]{2,1,0:T(8,128)(2,1)}), bf16[64,5,256]{2,1,0:T(8,128)(2,1)S(1)}, u32[]{:S(2)}, u32[]{:S(2)}) %all-to-all-start.8) | async-done | bytes 163872 | tf_op jit(solution)/shard_map/all_to_all | solution.py:109
  357.2 1.0 gather_fusion
  358.2 0.8 fusion.4
  (57 shorter events, 1.2 us)
Async XLA Ops:
  7.2 29.1 %copy-start.5 = (bf16[1,2048,128]{2,1,0:T(8,128)(2,1)S(1)}, bf16[1,2048,128]{2,1,0:T(8,128)(2,1)}, u32[]{:S(2)}) copy-start(bf16[1,2048,128]{2,1,0:T(8,128)(2,1)} %param.17) | copy-start | bytes 1572868
  36.3 29.8 %copy-start.12 = (s32[32,8]{0,1:T(8,128)S(1)}, s32[32,8]{0,1:T(8,128)}, u32[]{:S(2)}) copy-start(s32[32,8]{0,1:T(8,128)} %param.14) | copy-start | bytes 3076
  36.3 30.1 %copy-start.16 = (s32[64]{0:T(128)S(1)}, s32[64]{0:T(128)}, u32[]{:S(2)}) copy-start(s32[64]{0:T(128)} %param.16) | copy-start | bytes 772
  59.8 23.6 %all-to-all-start.1 = ((bf16[1,64,32,128]{3,2,0,1:T(8,128)(2,1)}), bf16[1,64,32,128]{3,2,0,1:T(8,128)(2,1)S(1)}, u32[]{:S(2)}, u32[]{:S(2)}) async-start(bf16[1,64,32,128]{3,2,0,1:T(8,128)(2,1)} %bitcast.3), calls=%async_computation.1 | async-start | bytes 1048576 | tf_op jit(solution)/shard_map/all_to_all | solution.py:14
  85.4 7.3 %copy-start.8 = (bf16[32,256]{1,0:T(8,128)(2,1)S(1)}, bf16[32,256]{1,0:T(8,128)(2,1)}, u32[]{:S(2)}) copy-start(bf16[32,256]{1,0:T(8,128)(2,1)} %param.12) | copy-start | bytes 49156
  85.4 35.5 %all-to-all-start.7 = ((bf16[1,64,32,128]{3,2,0,1:T(8,128)(2,1)}), bf16[1,64,32,128]{3,2,0,1:T(8,128)(2,1)S(1)}, u32[]{:S(2)}, u32[]{:S(2)}) async-start(bf16[1,64,32,128]{3,2,0,1:T(8,128)(2,1)} %get-tuple-element.11), calls=%async_computation.7 | async-start | bytes 1048576 | tf_op jit(solution)/shard_map/all_to_all | solution.py:12
  118.9 0.6 copy-start.10
  119.5 64.5 %copy-start.14 = (s32[256,1]{0,1:T(1,128)}, s32[256,1]{0,1:T(1,128)S(1)}, u32[]{:S(2)}) copy-start(s32[256,1]{0,1:T(1,128)S(1)} %compare_select_fusion.1) | copy-start | bytes 3076
  120.9 15.2 %copy-start = (bf16[1,64,32,128]{3,2,0,1:T(8,128)(2,1)}, bf16[1,64,32,128]{3,2,0,1:T(8,128)(2,1)S(1)}, u32[]{:S(2)}) copy-start(bf16[1,64,32,128]{3,2,0,1:T(8,128)(2,1)S(1)} %all-to-all-done.7) | copy-start | bytes 1572868
  120.9 32.5 %all-to-all-start.5 = ((bf16[1,64,32,128]{3,2,0,1:T(8,128)(2,1)}), bf16[1,64,32,128]{3,2,0,1:T(8,128)(2,1)S(1)}, u32[]{:S(2)}, u32[]{:S(2)}) async-start(bf16[1,64,32,128]{3,2,0,1:T(8,128)(2,1)} %get-tuple-element.10), calls=%async_computation.5 | async-start | bytes 1048576 | tf_op jit(solution)/shard_map/all_to_all | solution.py:13
  140.4 20.1 %copy-start.9 = (bf16[32,256]{1,0:T(8,128)(2,1)S(1)}, bf16[32,256]{1,0:T(8,128)(2,1)}, u32[]{:S(2)}) copy-start(bf16[32,256]{1,0:T(8,128)(2,1)} %param.13) | copy-start | bytes 49156
  153.4 0.8 copy-start.2
  154.2 57.5 %all-to-all-start.3 = ((bf16[64,5,2048]{2,1,0:T(8,128)(2,1)}), bf16[64,5,2048]{2,1,0:T(8,128)(2,1)S(1)}, u32[]{:S(2)}, u32[]{:S(2)}) async-start(bf16[64,5,2048]{2,1,0:T(8,128)(2,1)} %all_to_all.76), calls=%async_computation.3 | async-start | bytes 4194304 | tf_op jit(solution)/shard_map/all_to_all | solution.py:99
  180.8 3.0 copy-start.13
  268.9 23.3 %all-to-all-start.2 = ((bf16[1,64,32,128]{3,2,0,1:T(8,128)(2,1)}), bf16[1,64,32,128]{3,2,0,1:T(8,128)(2,1)}, u32[]{:S(2)}, u32[]{:S(2)}) async-start(bf16[1,64,32,128]{3,2,0,1:T(8,128)(2,1)} %get-tuple-element.12), calls=%async_computation.2 | async-start | bytes 1048576 | tf_op jit(solution)/shard_map/all_to_all | solution.py:14
  274.9 53.9 %reduce-scatter.2.cloned.1.call-start = ((), (), s32[]{:S(2)}) async-start(), calls=%async_computation.10 | async-start | bytes 1474560 | tf_op jit(solution)/shard_map/reduce_scatter | solution.py:106
  275.6 2.7 copy-start.1
  278.2 1.0 copy-start.3
  293.7 0.6 copy-start.6
  293.7 1.1 copy-start.4
  296.4 0.7 copy-start.11
  296.4 0.7 copy-start.15
  297.2 48.0 %copy-start.7 = (bf16[320,128]{1,0:T(8,128)(2,1)S(1)}, bf16[320,128]{1,0:T(8,128)(2,1)}, u32[]{:S(2)}) copy-start(bf16[320,128]{1,0:T(8,128)(2,1)} %copy-done.6) | copy-start | bytes 245764
  330.5 26.7 %all-to-all-start.8 = ((bf16[64,5,256]{2,1,0:T(8,128)(2,1)}), bf16[64,5,256]{2,1,0:T(8,128)(2,1)S(1)}, u32[]{:S(2)}, u32[]{:S(2)}) async-start(bf16[64,5,256]{2,1,0:T(8,128)(2,1)} %all_to_all.85), calls=%async_computation.9 | async-start | bytes 524288 | tf_op jit(solution)/shard_map/all_to_all | solution.py:109
Sparse Core Ops, SparseCore 0:
  296.6 32.1 reduce-scatter.1
where the time goes:
time: 367 us; the launch traced here: 366 us
  blocking collectives  156 us (43%)
  waiting for transfers between devices  103 us (28%)
  starting transfers between devices  54.9 us (15%)
  local copies, waits for them, and re-layouts  23.3 us (6%)
  between operations  14.4 us (4%)
  matrix products  9.47 us (3%)
  other arithmetic  4.82 us (1%)
    all_to_all x1, blocking collectives, local(): lax.all_to_all(grads, 'expert', split_axis=0, concat_axis=0, tiled=True)  57.2 us
    reduce_scatter x1, waiting for transfers between devices, local(): lax.psum_scatter(partial_value, 'dp', scatter_dimension=1, tiled=True)  30 us
    all_to_all x1, blocking collectives, relay_weights(): lax.all_to_all(second, 'expert', split_axis=1, concat_axis=0, tiled=True)  29.1 us
    all_to_all x2, waiting for transfers between devices, relay_weights(): lax.all_to_all(third, 'expert', split_axis=1, concat_axis=0, tiled=True)  28.1 us
    all_gather x1, blocking collectives, local(): lax.all_gather(tokens, 'dp', axis=1, tiled=True)  26.1 us
    all_to_all x1, blocking collectives, relay_weights(): lax.all_to_all(first, 'expert', split_axis=1, concat_axis=0, tiled=True)  23.5 us
    all_to_all x1, waiting for transfers between devices, local(): lax.all_to_all(inputs, 'expert', split_axis=0, concat_axis=0, tiled=True)  22.9 us
    all_gather x1, blocking collectives, local(): lax.all_gather(cotangent, 'dp', axis=1, tiled=True)  20.2 us
  transfers between devices with their start and end apart: 7, of which 6 were waited for; matrix products, arithmetic and copies ran while one was open for 5% of the time, Pallas kernels for 0%

commit v1 on v0

v1 whole, which is shorter than its diff:
```python
import jax
import jax.numpy as jnp
from jax import lax
from jax.experimental import pallas as pl
from jax.experimental.pallas import tpu as pltpu
from jax.sharding import PartitionSpec as P

BF = jnp.bfloat16
F32 = jnp.float32
CAP = 5
MIB = 1024 * 1024

contract_rows = (((0,), (0,)), ((), ()))
contract_cols = (((1,), (1,)), ((), ()))


def params():
    return pltpu.CompilerParams(vmem_limit_bytes=40 * MIB)


def vmem(n):
    return [pl.BlockSpec(memory_space=pltpu.VMEM)] * n


def dot(a, b, dims=(((1,), (0,)), ((), ()))):
    return lax.dot_general(a, b, dims, preferred_element_type=F32)


def pack_kernel(tok_ref, cot_ref, routes_ref, probs_ref, match_ref, send_ref, pick_ref):
    dests = match_ref.shape[1]
    rows = tok_ref.shape[0]
    width = tok_ref.shape[1]
    eye = lax.broadcasted_iota(jnp.int32, (dests, dests), 0) == lax.broadcasted_iota(
        jnp.int32, (dests, dests), 1
    )
    wanted = jnp.sum(jnp.where(eye, match_ref[...], 0), axis=1, keepdims=True)
    named = jnp.zeros((dests, rows), F32)
    weight = jnp.zeros((dests, rows), F32)
    for k in range(routes_ref.shape[0]):
        hit = wanted == routes_ref[k : k + 1, :]
        named = named + jnp.where(hit, 1.0, 0.0)
        weight = weight + jnp.where(hit, probs_ref[k : k + 1, :], 0.0)
    before = lax.broadcasted_iota(jnp.int32, (rows, rows), 0) < lax.broadcasted_iota(
        jnp.int32, (rows, rows), 1
    )
    rank = dot(named.astype(BF), jnp.where(before, 1.0, 0.0).astype(BF))
    for c in range(CAP):
        pick = jnp.where((named > 0.5) & (jnp.abs(rank - c) < 0.5), 1.0, 0.0)
        scale = jnp.sum(pick * weight, axis=1, keepdims=True)
        pick = pick.astype(BF)
        pick_ref[c * dests : (c + 1) * dests, :] = pick
        send_ref[:, c * width : (c + 1) * width] = dot(pick, tok_ref[...]).astype(BF)
        grads = dot(pick, cot_ref[...]) * scale
        send_ref[:, (CAP + c) * width : (CAP + c + 1) * width] = grads.astype(BF)


def pack(tokens, cotangent, routes, probs, matching):
    dests = matching.shape[0]
    rows, width = tokens.shape
    return pl.pallas_call(
        pack_kernel,
        out_shape=(
            jax.ShapeDtypeStruct((dests, 2 * CAP * width), BF),
            jax.ShapeDtypeStruct((CAP * dests, rows), BF),
        ),
        in_specs=vmem(5),
        out_specs=tuple(vmem(2)),
        compiler_params=params(),
    )(tokens, cotangent, routes.T, probs.T, matching.reshape(1, dests))


def reorder_kernel(match_ref, src_ref, dst_ref, sems):
    count, rows = dst_ref.shape[0], dst_ref.shape[1]
    copies = [
        pltpu.make_async_copy(
            src_ref.at[match_ref[d], pl.ds(0, rows)], dst_ref.at[d], sems.at[d]
        )
        for d in range(count)
    ]
    for c in copies:
        c.start()
    for c in copies:
        c.wait()


def reorder(arrived, matching, rows):
    count, _, lanes = arrived.shape
    return pl.pallas_call(
        reorder_kernel,
        out_shape=jax.ShapeDtypeStruct((count, rows, lanes), BF),
        in_specs=[
            pl.BlockSpec(memory_space=pltpu.SMEM),
            pl.BlockSpec(memory_space=pl.ANY),
        ],
        out_specs=pl.BlockSpec(memory_space=pl.ANY),
        scratch_shapes=[pltpu.SemaphoreType.DMA((count,))],
        compiler_params=params(),
        cost_estimate=pl.CostEstimate(
            flops=0, bytes_accessed=4 * count * rows * lanes, transcendentals=0
        ),
    )(matching, arrived)


def stack_slots(block, first, width):
    return jnp.concatenate(
        [block[:, (first + c) * width : (first + c + 1) * width] for c in range(CAP)], axis=0
    )


def expert_kernel(rows_ref, w_ref, back_ref, pair_ref, hidden_ref):
    slices, sources, _ = rows_ref.shape
    width = rows_ref.shape[2] // (2 * CAP)
    per = w_ref.shape[0] // slices
    part = w_ref.shape[1] // 3
    lanes = w_ref.shape[2]

    def weight(z, which):
        return w_ref[z * per : (z + 1) * per, which * part : (which + 1) * part, :].reshape(
            per * part, lanes
        )

    def both(z):
        return jnp.concatenate([weight(z, 0), weight(z, 1)], axis=1)

    two = jnp.zeros((CAP * sources, 2 * lanes), F32)
    hidden_back = jnp.zeros((CAP * sources, lanes), F32)
    for z in range(slices):
        block = rows_ref[z]
        two = two + dot(stack_slots(block, 0, width), both(z))
        hidden_back = hidden_back + dot(stack_slots(block, CAP, width), weight(z, 2))
    gate, upper = two[:, :lanes], two[:, lanes:]
    sig = jax.nn.sigmoid(gate)
    hidden_ref[...] = (gate * sig * upper).astype(BF)
    up_back = (hidden_back * gate * sig).astype(BF)
    gate_back = (hidden_back * upper * sig * (1.0 + gate * (1.0 - sig))).astype(BF)
    pair = jnp.concatenate([gate_back, up_back], axis=1)
    pair_ref[...] = pair
    for z in range(slices):
        parts = dot(pair, both(z), contract_cols).astype(BF)
        for c in range(CAP):
            back_ref[z, :, c * width : (c + 1) * width] = parts[c * sources : (c + 1) * sources, :]


def expert(rows, weights):
    slices, sources, lanes = rows.shape
    hidden = weights.shape[2]
    return pl.pallas_call(
        expert_kernel,
        out_shape=(
            jax.ShapeDtypeStruct((slices, sources, lanes // 2), BF),
            jax.ShapeDtypeStruct((CAP * sources, 2 * hidden), BF),
            jax.ShapeDtypeStruct((CAP * sources, hidden), BF),
        ),
        in_specs=vmem(2),
        out_specs=tuple(vmem(3)),
        compiler_params=params(),
    )(rows, weights)


def outer_kernel(rows_ref, pair_ref, hidden_ref, gate_ref, up_ref, down_ref):
    width = rows_ref.shape[2] // (2 * CAP)
    lanes = hidden_ref.shape[1]
    block = rows_ref[0]
    two = dot(stack_slots(block, 0, width), pair_ref[...], contract_rows)
    gate_ref[0] = two[:, :lanes]
    up_ref[0] = two[:, lanes:]
    down_ref[0] = dot(stack_slots(block, CAP, width), hidden_ref[...], contract_rows)


def outer(rows, pair, hidden):
    slices, sources, lanes = rows.shape
    width = lanes // (2 * CAP)
    units = hidden.shape[1]
    out = jax.ShapeDtypeStruct((1, slices * width, units), F32)
    flops = 2 * CAP * sources * slices * width * units * 3
    return pl.pallas_call(
        outer_kernel,
        grid=(slices,),
        out_shape=(out,) * 3,
        in_specs=[
            pl.BlockSpec((1, sources, lanes), lambda z: (z, 0, 0)),
            pl.BlockSpec(pair.shape, lambda z: (0, 0)),
            pl.BlockSpec(hidden.shape, lambda z: (0, 0)),
        ],
        out_specs=(pl.BlockSpec((1, width, units), lambda z: (0, z, 0)),) * 3,
        compiler_params=params(),
        cost_estimate=pl.CostEstimate(
            flops=flops, bytes_accessed=rows.size * 2 + 12 * slices * width * units, transcendentals=0
        ),
    )(rows, pair, hidden)


def combine_kernel(back_ref, pick_ref, out_ref):
    slices = back_ref.shape[0]
    width = out_ref.shape[1]
    pick = pick_ref[...]
    total = jnp.zeros(out_ref.shape, F32)
    for z in range(slices):
        total = total + dot(pick, stack_slots(back_ref[z], 0, width), contract_rows)
    out_ref[...] = total.astype(BF)


def combine(back, pick, shape):
    return pl.pallas_call(
        combine_kernel,
        out_shape=jax.ShapeDtypeStruct(shape, BF),
        in_specs=vmem(2),
        out_specs=pl.BlockSpec(memory_space=pltpu.VMEM),
        compiler_params=params(),
    )(back, pick)


def swap(x, axes):
    return lax.all_to_all(x, axes, split_axis=0, concat_axis=0, tiled=True)


def local(tokens, cotangent, routes, probs, matching, gate_weight, up_weight, down_weight):
    experts = matching.shape[0]
    model_width, units = gate_weight.shape[1:]
    slices = model_width // tokens.shape[1]
    piece = model_width // experts
    send, pick = pack(tokens, cotangent, routes, probs, matching)
    lanes = send.shape[1]
    first = jnp.concatenate(
        [w.reshape(experts, piece, units) for w in (gate_weight, up_weight, down_weight)]
        + [send.reshape(experts, lanes // units, units)],
        axis=1,
    )
    arrived = swap(first, "expert")
    rows = arrived[:, 3 * piece :, :].reshape(1, experts, lanes)
    rows = lax.all_gather(rows, "dp", axis=0, tiled=True)
    weights = swap(reorder(arrived, matching, 3 * piece), "expert")
    back, pair, hidden = expert(rows, weights)
    back = swap(back.reshape(slices * experts, 2, lanes // 4), ("dp", "expert"))
    gate_sum, up_sum, down_sum = outer(rows, pair, hidden)
    total = combine(back.reshape(slices, experts, lanes // 2), pick, tokens.shape)
    return (total, gate_sum, up_sum, down_sum)


def solution(mesh):
    placed = (
        P("expert", "dp"),
        P("expert", "dp"),
        P("expert", None),
        P("expert", None),
        P(),
        P("expert", None, "dp"),
        P("expert", None, "dp"),
        P("expert", None, "dp"),
    )
    return jax.shard_map(
        local,
        mesh=mesh,
        in_specs=placed,
        out_specs=(
            P("expert", "dp"),
            P("expert", None, "dp"),
            P("expert", None, "dp"),
            P("expert", None, "dp"),
        ),
        check_vma=False,
    )
```

time: 367 us -> 195 us (0.53)
  waiting for transfers between devices: 103 us -> 33 us
  blocking collectives: 156 us -> 105 us
  starting transfers between devices: 54.9 us -> 18.5 us
  local copies, waits for them, and re-layouts: 23.3 us -> 11 us
  Pallas kernels: 0 us -> 10.7 us
  matrix products: 9.47 us -> 0 us
    all_gather x2 -> x0, blocking collectives: 46.3 us -> none  [the longest x1 26.1 us: local(): lax.all_gather(tokens, 'dp', axis=1, tiled=True)]
    all_to_all x6 -> x1, waiting for transfers between devices: 72.8 us -> 32.9 us  [swap(): return lax.all_to_all(x, axes, split_axis=0, concat_axis=0, tiled=True)]
    all_to_all x6 -> x1, starting transfers between devices: 54.8 us -> 18.5 us  [swap(): return lax.all_to_all(x, axes, split_axis=0, concat_axis=0, tiled=True)]
    reduce_scatter x1 -> x0, waiting for transfers between devices: 30 us -> none  [local(): lax.psum_scatter(partial_value, 'dp', scatter_dimension=1, tiled=True)]
    pallas_call x0 -> x5, Pallas kernels: none -> 10.7 us  [the longest x1 4.55 us: outer(): pl.pallas_call(outer_kernel, grid=(slices,), out_shape=(out,) * 3, in_spe...]
    dot_general x8 -> x0, matrix products: 9.47 us -> none  [the longest x1 1.61 us: expert_grads(): lax.dot_general(inputs, gate_back, contract_rows, preferred_element_type=...]
    gather x6 -> x0, local copies, waits for them, and re-layouts: 8.39 us -> none  [the longest x1 3.01 us: build_rows(): jnp.take(jnp.concatenate([cotangent, blank], axis=0), slot_token, axis=0)]
    all_to_all x5 -> x0, local copies, waits for them, and re-layouts: 8.1 us -> none  [the longest x2 4.21 us: local(): lax.all_to_all(grads, 'expert', split_axis=0, concat_axis=0, tiled=True)]
  transfers between devices with their start and end apart: 7 -> 2, of which waited for: 6 -> 1; matrix products, arithmetic and copies ran while one was open for 5% -> 0% of each run, Pallas kernels for 0% -> 4%
where the time goes in v1:
time: 195 us; the launch traced here: 194 us
  blocking collectives  105 us (54%)
  waiting for transfers between devices  33 us (17%)
  starting transfers between devices  18.5 us (9%)
  between operations  14.1 us (7%)
  local copies, waits for them, and re-layouts  11 us (6%)
  Pallas kernels  10.7 us (5%)
    all_to_all x2, blocking collectives, swap(): return lax.all_to_all(x, axes, split_axis=0, concat_axis=0, tiled=True)  105 us
    all_to_all x1, waiting for transfers between devices, swap(): return lax.all_to_all(x, axes, split_axis=0, concat_axis=0, tiled=True)  32.9 us
    all_to_all x1, starting transfers between devices, swap(): return lax.all_to_all(x, axes, split_axis=0, concat_axis=0, tiled=True)  18.5 us
    unnamed x16, local copies, waits for them, and re-layouts  5.21 us
    pallas_call x1, Pallas kernels, outer(): pl.pallas_call(outer_kernel, grid=(slices,), out_shape=(out,) * 3, in_spe...  4.55 us
  transfers between devices with their start and end apart: 2, of which 1 were waited for; matrix products, arithmetic and copies ran while one was open for 0% of the time, Pallas kernels for 4%

profile of v1, /device:TPU:1, one launch (start us, length us, event | category | flops | bytes accessed | tf_op | source)
XLA Modules:
  0.0 194.1 jit_solution(5618010502074899457)
XLA Ops:
  7.2 0.0 all-gather.2.cloned.1.call-start
  7.2 0.0 copy-start.2
  7.2 0.7 copy-done.2
  7.9 0.0 copy-start.3
  7.9 0.7 copy-done.3
  8.6 0.0 copy-start.4
  8.7 0.7 copy-done.4
  9.3 0.0 copy-start.5
  9.3 0.7 copy-done.5
  10.0 0.0 copy-start.6
  10.0 0.7 copy-done.6
  10.7 0.5 shard_map.111
  11.2 0.2 reshape.36
  11.4 1.5 pad_maximum_fusion
  12.9 0.0 copy-start.7
  12.9 59.6 %all_to_all.15.src_ref = bf16[64,116,128]{2,1,0:T(8,128)(2,1)S(1)} all-to-all(bf16[64,116,128]{2,1,0:T(8,128)(2,1)S(1)} %pad_maximum_fusion), channel_id=1, replica_groups=mesh['dp'=8,'expert'=64] {'expert'}, dimensions={0} | all-to-all | bytes 3801088 | tf_op jit(solution)/shard_map/all_to_all | solution.py:214
  72.6 0.9 reshape.37
  73.5 0.0 all-gather.2.cloned.1.call-update
  73.5 0.0 copy-done.7
  73.5 3.5 %shard_map.112 = bf16[64,96,128]{2,1,0:T(8,128)(2,1)S(1)} custom-call(s32[64]{0:T(128)S(1)} %copy-done.7, bf16[64,116,128]{2,1,0:T(8,128)(2,1)S(1)} %all_to_all.15.src_ref), custom_call_target="tpu_custom_call" | custom-call | bytes 3145728 | tf_op jit(solution)/shard_map/pallas_call | solution.py:88
  77.0 45.6 %all_to_all.16.w_ref = bf16[64,96,128]{2,1,0:T(8,128)(2,1)S(1)} all-to-all(bf16[64,96,128]{2,1,0:T(8,128)(2,1)S(1)} %shard_map.112), channel_id=1, replica_groups=mesh['dp'=8,'expert'=64] {'expert'}, dimensions={0} | all-to-all | bytes 3145728 | tf_op jit(solution)/shard_map/all_to_all | solution.py:214
  122.7 0.0 all-gather.2.cloned.1.call-done.rows_ref
  122.7 0.0 copy-start
  122.7 1.7 copy-done
  124.4 1.2 shard_map.113
  125.7 1.2 reshape.38
  126.9 0.0 copy-start.1
  126.9 18.5 %all-to-all-start.2 = ((bf16[512,2,640]{2,1,0:T(2,128)(2,1)}), bf16[512,2,640]{2,1,0:T(2,128)(2,1)}, u32[]{:S(2)}, u32[]{:S(2)}) async-start(bf16[512,2,640]{2,1,0:T(2,128)(2,1)} %reshape.38), calls=%async_computation.2 | async-start | bytes 2621440 | tf_op jit(solution)/shard_map/all_to_all | solution.py:214
  145.4 0.0 copy-done.1
  145.4 4.5 %shard_map.115 = (f32[1,2048,128]{2,1,0:T(8,128)}, f32[1,2048,128]{2,1,0:T(8,128)}, f32[1,2048,128]{2,1,0:T(8,128)}) custom-call(bf16[8,64,2560]{2,1,0:T(8,128)(2,1)S(1)} %copy-done.1, bf16[320,256]{1,0:T(8,128)(2,1)S(1)} %get-tuple-element.15.pair_ref, bf16[320,128]{1,0:T(8,128)(2,1)S(1)} %get-tuple-element.16.hidden_ref), custom_call_target="tpu_custom_call" | custom-call | flops 503316480 | bytes 5767168 | tf_op jit(solution)/shard_map/pallas_call | solution.py:176
  150.0 32.9 %all-to-all-done.2 = bf16[512,2,640]{2,1,0:T(2,128)(2,1)} async-done(((bf16[512,2,640]{2,1,0:T(2,128)(2,1)}), bf16[512,2,640]{2,1,0:T(2,128)(2,1)}, u32[]{:S(2)}, u32[]{:S(2)}) %all-to-all-start.2) | async-done | bytes 1310752 | tf_op jit(solution)/shard_map/all_to_all | solution.py:214
  182.9 3.4 %reshape.39.back_ref = bf16[8,64,1280]{2,1,0:T(8,128)(2,1)S(1)} reshape(bf16[512,2,640]{2,1,0:T(2,128)(2,1)} %all-to-all-done.2) | data formatting | bytes 2621440 | tf_op jit(solution)/shard_map/reshape | solution.py:236
  186.3 1.0 shard_map.114
  (1 shorter events, 0.0 us)
Async XLA Ops:
  7.2 115.5 %all-gather.2.cloned.1.call-start = ((), (), s32[]{:S(2)}) async-start(), calls=%async_computation.3 | async-start | bytes 2949120 | tf_op jit(solution)/shard_map/all_gather | solution.py:231
  7.2 0.7 copy-start.2
  7.9 0.7 copy-start.3
  8.6 0.7 copy-start.4
  9.3 0.7 copy-start.5
  10.0 0.7 copy-start.6
  12.9 60.6 %copy-start.7 = (s32[64]{0:T(128)S(1)}, s32[64]{0:T(128)}, u32[]{:S(2)}) copy-start(s32[64]{0:T(128)} %match_ref.1) | copy-start | bytes 772
  122.7 1.7 copy-start
  126.9 18.5 %copy-start.1 = (bf16[8,64,2560]{2,1,0:T(8,128)(2,1)S(1)}, bf16[8,64,2560]{2,1,0:T(8,128)(2,1)}, u32[]{:S(2)}) copy-start(bf16[8,64,2560]{2,1,0:T(8,128)(2,1)} %all-gather.2.cloned.1.call-done.rows_ref) | copy-start | bytes 7864324
  126.9 56.0 %all-to-all-start.2 = ((bf16[512,2,640]{2,1,0:T(2,128)(2,1)}), bf16[512,2,640]{2,1,0:T(2,128)(2,1)}, u32[]{:S(2)}, u32[]{:S(2)}) async-start(bf16[512,2,640]{2,1,0:T(2,128)(2,1)} %reshape.38), calls=%async_computation.2 | async-start | bytes 2621440 | tf_op jit(solution)/shard_map/all_to_all | solution.py:214
Sparse Core Ops, SparseCore 0:
  73.6 42.7 all-gather.1

commit v2 on v1

--- a/solution.py
+++ b/solution.py
@@ -26,7 +26,23 @@
     return lax.dot_general(a, b, dims, preferred_element_type=F32)
 
 
-def pack_kernel(tok_ref, cot_ref, routes_ref, probs_ref, match_ref, send_ref, pick_ref):
+def pack_kernel(
+    tok_hbm, cot_hbm, routes_hbm, probs_hbm, match_hbm,
+    send_ref, pick_ref,
+    tok_ref, cot_ref, routes_ref, probs_ref, match_ref, sems,
+):
+    pairs = (
+        (routes_hbm, routes_ref),
+        (probs_hbm, probs_ref),
+        (match_hbm, match_ref),
+        (tok_hbm, tok_ref),
+        (cot_hbm, cot_ref),
+    )
+    copies = [pltpu.make_async_copy(a, b, sems.at[i]) for i, (a, b) in enumerate(pairs)]
+    for c in copies:
+        c.start()
+    for c in copies:
+        c.wait()
     dests = match_ref.shape[1]
     rows = tok_ref.shape[0]
     width = tok_ref.shape[1]
@@ -63,8 +79,16 @@
             jax.ShapeDtypeStruct((dests, 2 * CAP * width), BF),
             jax.ShapeDtypeStruct((CAP * dests, rows), BF),
         ),
-        in_specs=vmem(5),
+        in_specs=[pl.BlockSpec(memory_space=pltpu.HBM)] * 5,
         out_specs=tuple(vmem(2)),
+        scratch_shapes=[
+            pltpu.VMEM(tokens.shape, BF),
+            pltpu.VMEM(tokens.shape, BF),
+            pltpu.VMEM(routes.shape[::-1], jnp.int32),
+            pltpu.VMEM(routes.shape[::-1], F32),
+            pltpu.VMEM((1, dests), jnp.int32),
+            pltpu.SemaphoreType.DMA((5,)),
+        ],
         compiler_params=params(),
     )(tokens, cotangent, routes.T, probs.T, matching.reshape(1, dests))
 
@@ -136,9 +160,7 @@
     pair = jnp.concatenate([gate_back, up_back], axis=1)
     pair_ref[...] = pair
     for z in range(slices):
-        parts = dot(pair, both(z), contract_cols).astype(BF)
-        for c in range(CAP):
-            back_ref[z, :, c * width : (c + 1) * width] = parts[c * sources : (c + 1) * sources, :]
+        back_ref[z] = dot(pair, both(z), contract_cols).astype(BF)
 
 
 def expert(rows, weights):
@@ -147,7 +169,7 @@
     return pl.pallas_call(
         expert_kernel,
         out_shape=(
-            jax.ShapeDtypeStruct((slices, sources, lanes // 2), BF),
+            jax.ShapeDtypeStruct((slices, CAP * sources, lanes // (2 * CAP)), BF),
             jax.ShapeDtypeStruct((CAP * sources, 2 * hidden), BF),
             jax.ShapeDtypeStruct((CAP * sources, hidden), BF),
         ),
@@ -190,14 +212,32 @@
     )(rows, pair, hidden)
 
 
+def total_kernel(parts_ref, out_ref):
+    slices, rows, width = parts_ref.shape
+    sources = rows // CAP
+    total = parts_ref[0].astype(F32)
+    for z in range(1, slices):
+        total = total + parts_ref[z].astype(F32)
+    total = total.astype(BF)
+    for c in range(CAP):
+        out_ref[:, c * width : (c + 1) * width] = total[c * sources : (c + 1) * sources, :]
+
+
+def slice_total(parts):
+    _, rows, width = parts.shape
+    return pl.pallas_call(
+        total_kernel,
+        out_shape=jax.ShapeDtypeStruct((rows // CAP, CAP * width), BF),
+        in_specs=vmem(1),
+        out_specs=pl.BlockSpec(memory_space=pltpu.VMEM),
+        compiler_params=params(),
+    )(parts)
+
+
 def combine_kernel(back_ref, pick_ref, out_ref):
-    slices = back_ref.shape[0]
     width = out_ref.shape[1]
-    pick = pick_ref[...]
-    total = jnp.zeros(out_ref.shape, F32)
-    for z in range(slices):
-        total = total + dot(pick, stack_slots(back_ref[z], 0, width), contract_rows)
-    out_ref[...] = total.astype(BF)
+    rows = stack_slots(back_ref[...], 0, width)
+    out_ref[...] = dot(pick_ref[...], rows, contract_rows).astype(BF)
 
 
 def combine(back, pick, shape):
@@ -217,7 +257,6 @@
 def local(tokens, cotangent, routes, probs, matching, gate_weight, up_weight, down_weight):
     experts = matching.shape[0]
     model_width, units = gate_weight.shape[1:]
-    slices = model_width // tokens.shape[1]
     piece = model_width // experts
     send, pick = pack(tokens, cotangent, routes, probs, matching)
     lanes = send.shape[1]
@@ -231,9 +270,10 @@
     rows = lax.all_gather(rows, "dp", axis=0, tiled=True)
     weights = swap(reorder(arrived, matching, 3 * piece), "expert")
     back, pair, hidden = expert(rows, weights)
-    back = swap(back.reshape(slices * experts, 2, lanes // 4), ("dp", "expert"))
+    back = slice_total(swap(back, "dp"))
+    back = swap(back.reshape(experts, 2, lanes // 4), "expert")
     gate_sum, up_sum, down_sum = outer(rows, pair, hidden)
-    total = combine(back.reshape(slices, experts, lanes // 2), pick, tokens.shape)
+    total = combine(back.reshape(experts, lanes // 2), pick, tokens.shape)
     return (total, gate_sum, up_sum, down_sum)
 
 

time: 195 us -> 196 us (level)
  blocking collectives: 105 us -> 150 us
  waiting for transfers between devices: 33 us -> 6.05 us
  starting transfers between devices: 18.5 us -> 6.23 us
  local copies, waits for them, and re-layouts: 11 us -> 7.1 us
    all_to_all x2 -> x3, blocking collectives: 105 us -> 150 us  [swap(): return lax.all_to_all(x, axes, split_axis=0, concat_axis=0, tiled=True)]
    all_to_all x1, waiting for transfers between devices: 32.9 us -> 6.03 us  [swap(): return lax.all_to_all(x, axes, split_axis=0, concat_axis=0, tiled=True)]
    all_to_all x1, starting transfers between devices: 18.5 us -> 6.19 us  [swap(): return lax.all_to_all(x, axes, split_axis=0, concat_axis=0, tiled=True)]
    reshape x2 -> x1, local copies, waits for them, and re-layouts: 4.59 us -> 0.71 us  [local(): back = swap(back.reshape(experts, 2, lanes // 4), 'expert')]
    unnamed x16 -> x17, local copies, waits for them, and re-layouts: 5.21 us -> 5.23 us
where the time goes in v2:
time: 196 us
  blocking collectives  150 us (77%)
  between operations  14.1 us (7%)
  Pallas kernels  10.8 us (6%)
  local copies, waits for them, and re-layouts  7.1 us (4%)
  starting transfers between devices  6.23 us (3%)
  waiting for transfers between devices  6.05 us (3%)
    all_to_all x3, blocking collectives, swap(): return lax.all_to_all(x, axes, split_axis=0, concat_axis=0, tiled=True)  150 us
    all_to_all x1, starting transfers between devices, swap(): return lax.all_to_all(x, axes, split_axis=0, concat_axis=0, tiled=True)  6.19 us
    all_to_all x1, waiting for transfers between devices, swap(): return lax.all_to_all(x, axes, split_axis=0, concat_axis=0, tiled=True)  6.03 us
    unnamed x17, local copies, waits for them, and re-layouts  5.23 us
    pallas_call x1, Pallas kernels, outer(): pl.pallas_call(outer_kernel, grid=(slices,), out_shape=(out,) * 3, in_spe...  4.55 us
  transfers between devices with their start and end apart: 2, of which 1 were waited for; matrix products, arithmetic and copies ran while one was open for 0% of the time, Pallas kernels for 4%

profile of v2, /device:TPU:1, one launch (start us, length us, event | category | flops | bytes accessed | tf_op | source)
XLA Modules:
  0.0 196.0 jit_solution(11516402615010004318)
XLA Ops:
  7.2 0.0 all-gather.2.cloned.1.call-start
  7.2 0.0 copy-start.2
  7.2 0.7 copy-done.2
  7.9 0.0 copy-start.3
  7.9 0.7 copy-done.3
  8.6 0.0 copy-start.4
  8.7 0.7 copy-done.4
  9.3 0.0 copy-start.5
  9.3 0.7 copy-done.5
  10.0 0.0 copy-start.6
  10.0 0.7 copy-done.6
  10.7 0.6 shard_map.111
  11.2 0.2 reshape.36
  11.5 1.5 pad_maximum_fusion
  13.0 0.0 copy-start.7
  13.0 59.6 %all_to_all.20.src_ref = bf16[64,116,128]{2,1,0:T(8,128)(2,1)S(1)} all-to-all(bf16[64,116,128]{2,1,0:T(8,128)(2,1)S(1)} %pad_maximum_fusion), channel_id=1, replica_groups=mesh['dp'=8,'expert'=64] {'expert'}, dimensions={0} | all-to-all | bytes 3801088 | tf_op jit(solution)/shard_map/all_to_all | solution.py:254
  72.7 0.9 reshape.37
  73.6 0.0 all-gather.2.cloned.1.call-update
  73.6 0.0 copy-done.7
  73.6 3.5 %shard_map.112 = bf16[64,96,128]{2,1,0:T(8,128)(2,1)S(1)} custom-call(s32[64]{0:T(128)S(1)} %copy-done.7, bf16[64,116,128]{2,1,0:T(8,128)(2,1)S(1)} %all_to_all.20.src_ref), custom_call_target="tpu_custom_call" | custom-call | bytes 3145728 | tf_op jit(solution)/shard_map/pallas_call | solution.py:112
  77.1 45.6 %all_to_all.21.w_ref = bf16[64,96,128]{2,1,0:T(8,128)(2,1)S(1)} all-to-all(bf16[64,96,128]{2,1,0:T(8,128)(2,1)S(1)} %shard_map.112), channel_id=1, replica_groups=mesh['dp'=8,'expert'=64] {'expert'}, dimensions={0} | all-to-all | bytes 3145728 | tf_op jit(solution)/shard_map/all_to_all | solution.py:254
  122.8 0.0 all-gather.2.cloned.1.call-done.rows_ref
  122.8 0.0 copy-start
  122.8 1.7 copy-done
  124.5 1.3 shard_map.113
  125.8 0.0 copy-start.1
  125.8 44.8 %all_to_all.22.parts_ref = bf16[8,320,256]{2,1,0:T(8,128)(2,1)S(1)} all-to-all(bf16[8,320,256]{2,1,0:T(8,128)(2,1)S(1)} %get-tuple-element.13), channel_id=1, replica_groups=mesh['dp'=8,'expert'=64] {'dp'}, dimensions={0} | all-to-all | bytes 2621440 | tf_op jit(solution)/shard_map/all_to_all | solution.py:254
  170.6 0.2 shard_map.114
  170.8 0.7 reshape.38
  171.5 6.2 %all-to-all-start.3 = ((bf16[64,2,640]{2,1,0:T(2,128)(2,1)}), bf16[64,2,640]{2,1,0:T(2,128)(2,1)S(1)}, u32[]{:S(2)}, u32[]{:S(2)}) async-start(bf16[64,2,640]{2,1,0:T(2,128)(2,1)} %reshape.38), calls=%async_computation.3 | async-start | bytes 327680 | tf_op jit(solution)/shard_map/all_to_all | solution.py:254
  177.7 0.0 copy-done.1
  177.7 4.5 %shard_map.116 = (f32[1,2048,128]{2,1,0:T(8,128)}, f32[1,2048,128]{2,1,0:T(8,128)}, f32[1,2048,128]{2,1,0:T(8,128)}) custom-call(bf16[8,64,2560]{2,1,0:T(8,128)(2,1)S(1)} %copy-done.1, bf16[320,256]{1,0:T(8,128)(2,1)S(1)} %get-tuple-element.15.pair_ref, bf16[320,128]{1,0:T(8,128)(2,1)S(1)} %get-tuple-element.16.hidden_ref), custom_call_target="tpu_custom_call" | custom-call | flops 503316480 | bytes 5767168 | tf_op jit(solution)/shard_map/pallas_call | solution.py:198
  182.3 6.0 %all-to-all-done.3 = bf16[64,2,640]{2,1,0:T(2,128)(2,1)S(1)} async-done(((bf16[64,2,640]{2,1,0:T(2,128)(2,1)}), bf16[64,2,640]{2,1,0:T(2,128)(2,1)S(1)}, u32[]{:S(2)}, u32[]{:S(2)}) %all-to-all-start.3) | async-done | bytes 163872 | tf_op jit(solution)/shard_map/all_to_all | solution.py:254
  188.3 0.8 shard_map.115
  (2 shorter events, 0.1 us)
Async XLA Ops:
  7.2 115.6 %all-gather.2.cloned.1.call-start = ((), (), s32[]{:S(2)}) async-start(), calls=%async_computation.4 | async-start | bytes 2949120 | tf_op jit(solution)/shard_map/all_gather | solution.py:270
  7.2 0.7 copy-start.2
  7.9 0.7 copy-start.3
  8.6 0.7 copy-start.4
  9.3 0.7 copy-start.5
  10.0 0.7 copy-start.6
  13.0 60.6 %copy-start.7 = (s32[64]{0:T(128)S(1)}, s32[64]{0:T(128)}, u32[]{:S(2)}) copy-start(s32[64]{0:T(128)} %match_ref.1) | copy-start | bytes 772
  122.8 1.7 copy-start
  125.8 51.9 %copy-start.1 = (bf16[8,64,2560]{2,1,0:T(8,128)(2,1)S(1)}, bf16[8,64,2560]{2,1,0:T(8,128)(2,1)}, u32[]{:S(2)}) copy-start(bf16[8,64,2560]{2,1,0:T(8,128)(2,1)} %all-gather.2.cloned.1.call-done.rows_ref) | copy-start | bytes 7864324
  171.5 16.8 %all-to-all-start.3 = ((bf16[64,2,640]{2,1,0:T(2,128)(2,1)}), bf16[64,2,640]{2,1,0:T(2,128)(2,1)S(1)}, u32[]{:S(2)}, u32[]{:S(2)}) async-start(bf16[64,2,640]{2,1,0:T(2,128)(2,1)} %reshape.38), calls=%async_computation.3 | async-start | bytes 327680 | tf_op jit(solution)/shard_map/all_to_all | solution.py:254
Sparse Core Ops, SparseCore 0:
  73.7 42.7 all-gather.1

commit v3 on v2

v3 whole, which is shorter than its diff:
```python
import jax
import jax.numpy as jnp
from jax import lax
from jax.experimental import pallas as pl
from jax.experimental.pallas import tpu as pltpu
from jax.sharding import PartitionSpec as P

BF = jnp.bfloat16
F32 = jnp.float32
CAP = 5
MIB = 1024 * 1024

contract_rows = (((0,), (0,)), ((), ()))
contract_cols = (((1,), (1,)), ((), ()))


def params(whole=False):
    return pltpu.CompilerParams(vmem_limit_bytes=(63 if whole else 40) * MIB)


def vmem(n):
    return [pl.BlockSpec(memory_space=pltpu.VMEM)] * n


def dot(a, b, dims=(((1,), (0,)), ((), ()))):
    return lax.dot_general(a, b, dims, preferred_element_type=F32)


def pack_kernel(
    tok_hbm, cot_hbm, routes_hbm, probs_hbm, match_hbm,
    home_ref, away_ref, pick_ref,
    tok_ref, cot_ref, routes_ref, probs_ref, match_ref, sems,
):
    pairs = (
        (routes_hbm, routes_ref),
        (probs_hbm, probs_ref),
        (match_hbm, match_ref),
        (tok_hbm, tok_ref),
        (cot_hbm, cot_ref),
    )
    copies = [pltpu.make_async_copy(a, b, sems.at[i]) for i, (a, b) in enumerate(pairs)]
    for c in copies:
        c.start()
    for c in copies:
        c.wait()
    dests = match_ref.shape[1]
    rows = tok_ref.shape[0]
    width = tok_ref.shape[1]
    down = lax.broadcasted_iota(jnp.int32, (dests, dests), 0)
    across = lax.broadcasted_iota(jnp.int32, (dests, dests), 1)
    matched = jnp.sum(jnp.where(down == across, match_ref[...], 0), axis=1, keepdims=True)
    named = jnp.zeros((dests, rows), F32)
    weight = jnp.zeros((dests, rows), F32)
    experts = lax.broadcasted_iota(jnp.int32, (dests, rows), 0)
    for k in range(routes_ref.shape[0]):
        hit = experts == routes_ref[k : k + 1, :]
        named = named + jnp.where(hit, 1.0, 0.0)
        weight = weight + jnp.where(hit, probs_ref[k : k + 1, :], 0.0)
    before = lax.broadcasted_iota(jnp.int32, (rows, rows), 0) < lax.broadcasted_iota(
        jnp.int32, (rows, rows), 1
    )
    rank = dot(named.astype(BF), jnp.where(before, 1.0, 0.0).astype(BF))
    for c in range(CAP):
        pick = jnp.where((named > 0.5) & (jnp.abs(rank - c) < 0.5), 1.0, 0.0)
        scale = jnp.sum(pick * weight, axis=1, keepdims=True)
        pick = pick.astype(BF)
        pick_ref[c * dests : (c + 1) * dests, :] = pick
        home_ref[:, c * width : (c + 1) * width] = dot(pick, tok_ref[...]).astype(BF)
        grads = dot(pick, cot_ref[...]) * scale
        home_ref[:, (CAP + c) * width : (CAP + c + 1) * width] = grads.astype(BF)
    order = jnp.where(matched == across, 1.0, 0.0).astype(BF)
    away_ref[...] = dot(order, home_ref[...]).astype(BF)


def pack(tokens, cotangent, routes, probs, matching):
    dests = matching.shape[0]
    rows, width = tokens.shape
    buffer = jax.ShapeDtypeStruct((dests, 2 * CAP * width), BF)
    return pl.pallas_call(
        pack_kernel,
        out_shape=(buffer, buffer, jax.ShapeDtypeStruct((CAP * dests, rows), BF)),
        in_specs=[pl.BlockSpec(memory_space=pltpu.HBM)] * 5,
        out_specs=tuple(vmem(3)),
        scratch_shapes=[
            pltpu.VMEM(tokens.shape, BF),
            pltpu.VMEM(tokens.shape, BF),
            pltpu.VMEM(routes.shape[::-1], jnp.int32),
            pltpu.VMEM(routes.shape[::-1], F32),
            pltpu.VMEM((1, dests), jnp.int32),
            pltpu.SemaphoreType.DMA((5,)),
        ],
        compiler_params=params(whole=True),
    )(tokens, cotangent, routes.T, probs.T, matching.reshape(1, dests))


def stack_slots(block, first, width):
    return jnp.concatenate(
        [block[:, (first + c) * width : (first + c + 1) * width] for c in range(CAP)], axis=0
    )


def expert_kernel(rows_ref, gate_ref, up_ref, down_ref, send_ref):
    slices, sources, _ = rows_ref.shape
    width = rows_ref.shape[2] // (2 * CAP)
    lanes = gate_ref.shape[2]
    model = slices * width

    def both(z):
        part = slice(z * width, (z + 1) * width)
        return jnp.concatenate([gate_ref[0, part, :], up_ref[0, part, :]], axis=1)

    two = jnp.zeros((CAP * sources, 2 * lanes), F32)
    hidden_back = jnp.zeros((CAP * sources, lanes), F32)
    for z in range(slices):
        block = rows_ref[z]
        two = two + dot(stack_slots(block, 0, width), both(z))
        hidden_back = hidden_back + dot(
            stack_slots(block, CAP, width), down_ref[0, z * width : (z + 1) * width, :]
        )
    gate, upper = two[:, :lanes], two[:, lanes:]
    sig = jax.nn.sigmoid(gate)
    hidden = (gate * sig * upper).astype(BF)
    up_back = (hidden_back * gate * sig).astype(BF)
    gate_back = (hidden_back * upper * sig * (1.0 + gate * (1.0 - sig))).astype(BF)
    pair = jnp.concatenate([gate_back, up_back], axis=1)
    for z in range(slices):
        parts = dot(pair, both(z), contract_cols).astype(BF)
        for c in range(CAP):
            at = c * model + z * width
            send_ref[:, at : at + width] = parts[c * sources : (c + 1) * sources, :]
    for c in range(CAP):
        own = slice(c * sources, (c + 1) * sources)
        at = CAP * model + c * 3 * lanes
        send_ref[:, at : at + 2 * lanes] = pair[own, :]
        send_ref[:, at + 2 * lanes : at + 3 * lanes] = hidden[own, :]
    used = CAP * (model + 3 * lanes)
    send_ref[:, used:] = jnp.zeros((sources, send_ref.shape[1] - used), BF)


def expert(rows, w_gate, w_up, w_down):
    sources = rows.shape[1]
    model, units = w_gate.shape[1:]
    used = CAP * (model + 3 * units)
    return pl.pallas_call(
        expert_kernel,
        out_shape=jax.ShapeDtypeStruct((sources, -(-used // 1024) * 1024), BF),
        in_specs=vmem(4),
        out_specs=pl.BlockSpec(memory_space=pltpu.VMEM),
        compiler_params=params(),
    )(rows, w_gate, w_up, w_down)


def outer_kernel(rows_ref, factor_ref, gate_ref, up_ref, down_ref):
    width = rows_ref.shape[2] // (2 * CAP)
    lanes = gate_ref.shape[2]
    block = rows_ref[0]
    factors = stack_slots(factor_ref[...], 0, 3 * lanes)
    two = dot(stack_slots(block, 0, width), factors[:, : 2 * lanes], contract_rows)
    gate_ref[0] = two[:, :lanes]
    up_ref[0] = two[:, lanes:]
    down_ref[0] = dot(stack_slots(block, CAP, width), factors[:, 2 * lanes :], contract_rows)


def outer(rows, factors, units):
    slices, sources, lanes = rows.shape
    width = lanes // (2 * CAP)
    out = jax.ShapeDtypeStruct((1, slices * width, units), F32)
    flops = 2 * CAP * sources * slices * width * units * 3
    return pl.pallas_call(
        outer_kernel,
        grid=(slices,),
        out_shape=(out,) * 3,
        in_specs=[
            pl.BlockSpec((1, sources, lanes), lambda z: (z, 0, 0)),
            pl.BlockSpec(factors.shape, lambda z: (0, 0)),
        ],
        out_specs=(pl.BlockSpec((1, width, units), lambda z: (0, z, 0)),) * 3,
        compiler_params=params(whole=True),
        cost_estimate=pl.CostEstimate(
            flops=flops, bytes_accessed=rows.size * 2 + 12 * slices * width * units, transcendentals=0
        ),
    )(rows, factors)


def relay_kernel(back_ref, match_ref, out_ref):
    count = back_ref.shape[0]
    down = lax.broadcasted_iota(jnp.int32, (count, count), 0)
    across = lax.broadcasted_iota(jnp.int32, (count, count), 1)
    matched = jnp.sum(jnp.where(down == across, match_ref[...], 0), axis=1, keepdims=True)
    order = jnp.where(matched == across, 1.0, 0.0).astype(BF)
    out_ref[...] = dot(order, back_ref[:, back_ref.shape[1] - out_ref.shape[1] :]).astype(BF)


def relay(back, matching, lanes):
    count = back.shape[0]
    return pl.pallas_call(
        relay_kernel,
        out_shape=jax.ShapeDtypeStruct((count, lanes), BF),
        in_specs=vmem(2),
        out_specs=pl.BlockSpec(memory_space=pltpu.VMEM),
        compiler_params=params(),
    )(back, matching.reshape(1, count))


def combine_kernel(back_ref, pick_ref, out_ref):
    slices, _, width = out_ref.shape
    pick = pick_ref[...]
    for z in range(slices):
        rows = jnp.concatenate(
            [
                back_ref[:, (c * slices + z) * width : (c * slices + z + 1) * width]
                for c in range(CAP)
            ],
            axis=0,
        )
        out_ref[z] = dot(pick, rows, contract_rows).astype(BF)


def combine(back, pick, slices, width):
    rows = pick.shape[1]
    return pl.pallas_call(
        combine_kernel,
        out_shape=jax.ShapeDtypeStruct((slices, rows, width), BF),
        in_specs=vmem(2),
        out_specs=pl.BlockSpec(memory_space=pltpu.VMEM),
        compiler_params=params(),
        cost_estimate=pl.CostEstimate(
            flops=2 * pick.size * slices * width, bytes_accessed=2 * back.size, transcendentals=0
        ),
    )(back, pick)


def total_kernel(parts_ref, out_ref):
    total = parts_ref[0].astype(F32)
    for z in range(1, parts_ref.shape[0]):
        total = total + parts_ref[z].astype(F32)
    out_ref[...] = total.astype(BF)


def slice_total(parts):
    return pl.pallas_call(
        total_kernel,
        out_shape=jax.ShapeDtypeStruct(parts.shape[1:], BF),
        in_specs=vmem(1),
        out_specs=pl.BlockSpec(memory_space=pltpu.VMEM),
        compiler_params=params(),
    )(parts)


def swap(x, axes):
    return lax.all_to_all(x, axes, split_axis=0, concat_axis=0, tiled=True)


def spread(send):
    dests, lanes = send.shape
    rows = swap(send.reshape(dests, lanes // 128, 128), "expert").reshape(1, dests, lanes)
    return lax.all_gather(rows, "dp", axis=0, tiled=True)


def local(tokens, cotangent, routes, probs, matching, gate_weight, up_weight, down_weight):
    experts = matching.shape[0]
    model, units = gate_weight.shape[1:]
    width = tokens.shape[1]
    home, away, pick = pack(tokens, cotangent, routes, probs, matching)
    home_rows = spread(home)
    away_rows = spread(away)
    send = expert(home_rows, gate_weight, up_weight, down_weight)
    lanes = send.shape[1]
    back = swap(send.reshape(experts, lanes // 128, 128), "expert").reshape(experts, lanes)
    span = lanes - CAP * model
    moved = swap(relay(back, matching, span).reshape(experts, span // 128, 128), "expert")
    sums, moved = lax.optimization_barrier((combine(back, pick, model // width, width), moved))
    parts = swap(sums, "dp")
    gate_sum, up_sum, down_sum = outer(away_rows, moved.reshape(experts, span), units)
    return (slice_total(parts), gate_sum, up_sum, down_sum)


def solution(mesh):
    placed = (
        P("expert", "dp"),
        P("expert", "dp"),
        P("expert", None),
        P("expert", None),
        P(),
        P("expert", None, "dp"),
        P("expert", None, "dp"),
        P("expert", None, "dp"),
    )
    return jax.shard_map(
        local,
        mesh=mesh,
        in_specs=placed,
        out_specs=(
            P("expert", "dp"),
            P("expert", None, "dp"),
            P("expert", None, "dp"),
            P("expert", None, "dp"),
        ),
        check_vma=False,
    )
```

time: 196 us -> 177 us (0.903)
  blocking collectives: 150 us -> 100 us
  waiting for transfers between devices: 6.05 us -> 31.8 us
  starting transfers between devices: 6.23 us -> 9.97 us
    all_to_all x3, blocking collectives: 150 us -> 100 us  [swap(): return lax.all_to_all(x, axes, split_axis=0, concat_axis=0, tiled=True)]
    all_gather x1 -> x2, waiting for transfers between devices: 0.01 us -> 20.8 us  [spread(): return lax.all_gather(rows, 'dp', axis=0, tiled=True)]
    all_to_all x1 -> x2, waiting for transfers between devices: 6.03 us -> 11 us  [swap(): return lax.all_to_all(x, axes, split_axis=0, concat_axis=0, tiled=True)]
    all_to_all x1 -> x2, starting transfers between devices: 6.19 us -> 9.89 us  [swap(): return lax.all_to_all(x, axes, split_axis=0, concat_axis=0, tiled=True)]
    pallas_call x1, Pallas kernels: 4.55 us -> 7.02 us  [outer(): pl.pallas_call(outer_kernel, grid=(slices,), out_shape=(out,) * 3, in_spe...]
    unnamed x17 -> x18, local copies, waits for them, and re-layouts: 5.23 us -> 4.22 us
  transfers between devices with their start and end apart: 2 -> 4, of which waited for: 1 -> 2; matrix products, arithmetic and copies ran while one was open for 0% -> 2% of each run, Pallas kernels for 4% -> 5%
where the time goes in v3:
time: 177 us; the launch traced here: 176 us
  blocking collectives  100 us (56%)
  waiting for transfers between devices  31.8 us (18%)
  between operations  14.1 us (8%)
  Pallas kernels  12.3 us (7%)
  starting transfers between devices  9.97 us (6%)
  local copies, waits for them, and re-layouts  7.51 us (4%)
    all_to_all x3, blocking collectives, swap(): return lax.all_to_all(x, axes, split_axis=0, concat_axis=0, tiled=True)  100 us
    all_gather x2, waiting for transfers between devices, spread(): return lax.all_gather(rows, 'dp', axis=0, tiled=True)  20.8 us
    all_to_all x2, waiting for transfers between devices, swap(): return lax.all_to_all(x, axes, split_axis=0, concat_axis=0, tiled=True)  11 us
    all_to_all x2, starting transfers between devices, swap(): return lax.all_to_all(x, axes, split_axis=0, concat_axis=0, tiled=True)  9.89 us
    pallas_call x1, Pallas kernels, outer(): pl.pallas_call(outer_kernel, grid=(slices,), out_shape=(out,) * 3, in_spe...  7.02 us
    unnamed x18, local copies, waits for them, and re-layouts  4.22 us
  transfers between devices with their start and end apart: 4, of which 2 were waited for; matrix products, arithmetic and copies ran while one was open for 2% of the time, Pallas kernels for 5%

profile of v3, /device:TPU:1, one launch (start us, length us, event | category | flops | bytes accessed | tf_op | source)
XLA Modules:
  0.0 175.7 jit_solution(12597389806945192233)
XLA Ops:
  7.2 0.0 all-gather.3.cloned.1.call-start
  7.2 2.1 %shard_map.111 = (bf16[64,2560]{1,0:T(8,128)(2,1)}, bf16[64,2560]{1,0:T(8,128)(2,1)}, bf16[320,32]{1,0:T(8,128)(2,1)}) custom-call(bf16[32,256]{1,0:T(8,128)(2,1)} %tok_hbm.1, bf16[32,256]{1,0:T(8,128)(2,1)} %cot_hbm.1, s32[8,32]{1,0:T(8,128)} %bitcast.25, f32[8,32]{1,0:T(8,128)} %bitcast.26, s32[1,64]{1,0:T(1,128)} %bitcast.19), custom_call_target="tpu_custom_call" | custom-call | tf_op jit(solution)/shard_map/pallas_call | solution.py:79
  9.3 0.0 copy-start.6
  9.4 1.2 reshape.37
  10.6 26.0 %all_to_all.25 = bf16[64,20,128]{2,1,0:T(8,128)(2,1)S(1)} all-to-all(bf16[64,20,128]{2,1,0:T(8,128)(2,1)S(1)} %reshape.37), channel_id=1, replica_groups=mesh['dp'=8,'expert'=64] {'expert'}, dimensions={0} | all-to-all | bytes 655360 | tf_op jit(solution)/shard_map/all_to_all | solution.py:251
  36.6 0.9 reshape.38
  37.5 0.0 copy-start.1
  37.5 0.0 copy-start.2
  37.5 0.0 copy-start.3
  37.5 0.0 all-gather.3.cloned.1.call-update
  37.6 0.0 all-gather.5.cloned.1.call-start
  37.6 0.0 copy-done.6
  37.6 0.2 reshape.42
  37.8 20.7 %all_to_all.26 = bf16[64,20,128]{2,1,0:T(8,128)(2,1)S(1)} all-to-all(bf16[64,20,128]{2,1,0:T(8,128)(2,1)S(1)} %reshape.42), channel_id=1, replica_groups=mesh['dp'=8,'expert'=64] {'expert'}, dimensions={0} | all-to-all | bytes 655360 | tf_op jit(solution)/shard_map/all_to_all | solution.py:251
  58.6 0.9 reshape.43
  59.5 0.0 all-gather.5.cloned.1.call-update
  59.5 20.8 %all-gather.3.cloned.1.call-done.rows_ref = bf16[8,64,2560]{2,1,0:T(8,128)(2,1)} async-done(((bf16[1,64,2560]{2,1,0:T(8,128)(2,1)}), bf16[8,64,2560]{2,1,0:T(8,128)(2,1)}) %all-gather.3.cloned.1.call-update) | async-done | bytes 2621456 | tf_op jit(solution)/shard_map/all_gather | solution.py:257
  80.3 0.0 copy-done.1
  80.3 0.0 copy-done.2
  80.3 0.0 copy-done.3
  80.3 0.0 copy-start
  80.3 1.7 copy-done
  82.1 1.2 shard_map.112
  83.3 0.3 copy.12
  83.6 53.2 %all_to_all.27 = bf16[64,96,128]{2,1,0:T(8,128)(2,1)S(1)} all-to-all(bf16[64,96,128]{2,1,0:T(8,128)(2,1)S(1)} %bitcast.21), channel_id=1, replica_groups=mesh['dp'=8,'expert'=64] {'expert'}, dimensions={0} | all-to-all | bytes 3145728 | tf_op jit(solution)/shard_map/all_to_all | solution.py:251
  136.8 0.0 copy-start.5
  136.8 0.6 copy.18
  137.4 0.0 copy-start.4
  137.4 0.0 copy-done.5
  137.5 0.3 shard_map.114
  137.8 0.7 copy.14
  138.5 6.1 %all-to-all-start.2 = ((bf16[64,16,128]{2,1,0:T(8,128)(2,1)}), bf16[64,16,128]{2,1,0:T(8,128)(2,1)S(1)}, u32[]{:S(2)}, u32[]{:S(2)}) async-start(bf16[64,16,128]{2,1,0:T(8,128)(2,1)} %bitcast.8), calls=%async_computation.2 | async-start | bytes 524288 | tf_op jit(solution)/shard_map/all_to_all | solution.py:251
  144.6 0.0 copy-done.4
  144.6 1.0 shard_map.113
  145.7 11.0 %all-to-all-done.2 = bf16[64,16,128]{2,1,0:T(8,128)(2,1)S(1)} async-done(((bf16[64,16,128]{2,1,0:T(8,128)(2,1)}), bf16[64,16,128]{2,1,0:T(8,128)(2,1)S(1)}, u32[]{:S(2)}, u32[]{:S(2)}) %all-to-all-start.2) | async-done | bytes 262176 | tf_op jit(solution)/shard_map/all_to_all | solution.py:251
  156.6 3.8 %all-to-all-start.3 = ((bf16[8,32,256]{2,1,0:T(8,128)(2,1)}), bf16[8,32,256]{2,1,0:T(8,128)(2,1)S(1)}, u32[]{:S(2)}, u32[]{:S(2)}) async-start(bf16[8,32,256]{2,1,0:T(8,128)(2,1)} %shard_map.113), calls=%async_computation.3 | async-start | bytes 262144 | tf_op jit(solution)/shard_map/all_to_all | solution.py:251
  160.4 0.8 copy.19
  161.2 0.0 all-gather.5.cloned.1.call-done.rows_ref
  161.2 7.0 %shard_map.116 = (f32[1,2048,128]{2,1,0:T(8,128)}, f32[1,2048,128]{2,1,0:T(8,128)}, f32[1,2048,128]{2,1,0:T(8,128)}) custom-call(bf16[8,64,2560]{2,1,0:T(8,128)(2,1)} %all-gather.5.cloned.1.call-done.rows_ref, bf16[64,2048]{1,0:T(8,128)(2,1)} %bitcast.24), custom_call_target="tpu_custom_call" | custom-call | flops 503316480 | bytes 5767168 | tf_op jit(solution)/shard_map/pallas_call | solution.py:169
  168.2 0.0 all-to-all-done.3.parts_ref
  168.2 0.6 shard_map.115
Async XLA Ops:
  7.2 73.1 %all-gather.3.cloned.1.call-start = ((), (), s32[]{:S(2)}) async-start(), calls=%async_computation.5 | async-start | bytes 2949120 | tf_op jit(solution)/shard_map/all_gather | solution.py:257
  9.3 28.3 %copy-start.6 = (bf16[64,2560]{1,0:T(8,128)(2,1)S(1)}, bf16[64,2560]{1,0:T(8,128)(2,1)}, u32[]{:S(2)}) copy-start(bf16[64,2560]{1,0:T(8,128)(2,1)} %get-tuple-element.15) | copy-start | bytes 983044
  37.5 42.8 %copy-start.1 = (bf16[1,2048,128]{2,1,0:T(8,128)(2,1)S(1)}, bf16[1,2048,128]{2,1,0:T(8,128)(2,1)}, u32[]{:S(2)}) copy-start(bf16[1,2048,128]{2,1,0:T(8,128)(2,1)} %gate_ref.1) | copy-start | bytes 1572868
  37.5 42.8 %copy-start.2 = (bf16[1,2048,128]{2,1,0:T(8,128)(2,1)S(1)}, bf16[1,2048,128]{2,1,0:T(8,128)(2,1)}, u32[]{:S(2)}) copy-start(bf16[1,2048,128]{2,1,0:T(8,128)(2,1)} %up_ref.1) | copy-start | bytes 1572868
  37.5 42.8 %copy-start.3 = (bf16[1,2048,128]{2,1,0:T(8,128)(2,1)S(1)}, bf16[1,2048,128]{2,1,0:T(8,128)(2,1)}, u32[]{:S(2)}) copy-start(bf16[1,2048,128]{2,1,0:T(8,128)(2,1)} %down_ref.1) | copy-start | bytes 1572868
  37.6 123.6 %all-gather.5.cloned.1.call-start = ((), (), s32[]{:S(2)}) async-start(), calls=%async_computation.6 | async-start | bytes 2949120 | tf_op jit(solution)/shard_map/all_gather | solution.py:257
  80.3 1.7 copy-start
  136.8 0.7 copy-start.5
  137.4 7.2 %copy-start.4 = (bf16[320,32]{1,0:T(8,128)(2,1)S(1)}, bf16[320,32]{1,0:T(8,128)(2,1)}, u32[]{:S(2)}) copy-start(bf16[320,32]{1,0:T(8,128)(2,1)} %get-tuple-element.13.pick_ref) | copy-start | bytes 61444
  138.5 18.1 %all-to-all-start.2 = ((bf16[64,16,128]{2,1,0:T(8,128)(2,1)}), bf16[64,16,128]{2,1,0:T(8,128)(2,1)S(1)}, u32[]{:S(2)}, u32[]{:S(2)}) async-start(bf16[64,16,128]{2,1,0:T(8,128)(2,1)} %bitcast.8), calls=%async_computation.2 | async-start | bytes 524288 | tf_op jit(solution)/shard_map/all_to_all | solution.py:251
  156.6 11.6 %all-to-all-start.3 = ((bf16[8,32,256]{2,1,0:T(8,128)(2,1)}), bf16[8,32,256]{2,1,0:T(8,128)(2,1)S(1)}, u32[]{:S(2)}, u32[]{:S(2)}) async-start(bf16[8,32,256]{2,1,0:T(8,128)(2,1)} %shard_map.113), calls=%async_computation.3 | async-start | bytes 262144 | tf_op jit(solution)/shard_map/all_to_all | solution.py:251
Sparse Core Ops, SparseCore 0:
  37.7 42.5 all-gather.2
  83.0 43.7 all-gather.4

commit v4 on v3

v4 whole, which is shorter than its diff:
```python
import functools

import jax
import jax.numpy as jnp
from jax import lax
from jax.experimental import pallas as pl
from jax.experimental.pallas import tpu as pltpu
from jax.sharding import PartitionSpec as P

BF = jnp.bfloat16
F32 = jnp.float32
CAP = 5
MIB = 1024 * 1024
LANES = 128

contract_rows = (((0,), (0,)), ((), ()))
contract_cols = (((1,), (1,)), ((), ()))


def params(whole=False):
    return pltpu.CompilerParams(vmem_limit_bytes=(63 if whole else 40) * MIB)


def vmem(n):
    return [pl.BlockSpec(memory_space=pltpu.VMEM)] * n


def dot(a, b, dims=(((1,), (0,)), ((), ()))):
    return lax.dot_general(a, b, dims, preferred_element_type=F32)


def fold(block, scratch, out_ref):
    count, rows, _ = out_ref.shape
    for q in range(rows):
        scratch[pl.ds(q, count, stride=rows), :] = block(q)
    out_ref[...] = scratch[...].reshape(out_ref.shape).astype(BF)


def pack_kernel(
    tok_hbm, cot_hbm, routes_hbm, probs_hbm, match_hbm,
    home_ref, away_ref, pick_ref,
    tok_ref, cot_ref, routes_ref, probs_ref, match_ref, flat_ref, fold_ref, sems,
):
    pairs = (
        (routes_hbm, routes_ref),
        (probs_hbm, probs_ref),
        (match_hbm, match_ref),
        (tok_hbm, tok_ref),
        (cot_hbm, cot_ref),
    )
    copies = [pltpu.make_async_copy(a, b, sems.at[i]) for i, (a, b) in enumerate(pairs)]
    for c in copies:
        c.start()
    for c in copies:
        c.wait()
    dests = match_ref.shape[1]
    rows = tok_ref.shape[0]
    width = tok_ref.shape[1]
    down = lax.broadcasted_iota(jnp.int32, (dests, dests), 0)
    across = lax.broadcasted_iota(jnp.int32, (dests, dests), 1)
    matched = jnp.sum(jnp.where(down == across, match_ref[...], 0), axis=1, keepdims=True)
    named = jnp.zeros((dests, rows), F32)
    weight = jnp.zeros((dests, rows), F32)
    experts = lax.broadcasted_iota(jnp.int32, (dests, rows), 0)
    for k in range(routes_ref.shape[0]):
        hit = experts == routes_ref[k : k + 1, :]
        named = named + jnp.where(hit, 1.0, 0.0)
        weight = weight + jnp.where(hit, probs_ref[k : k + 1, :], 0.0)
    before = lax.broadcasted_iota(jnp.int32, (rows, rows), 0) < lax.broadcasted_iota(
        jnp.int32, (rows, rows), 1
    )
    rank = dot(named.astype(BF), jnp.where(before, 1.0, 0.0).astype(BF))
    for c in range(CAP):
        pick = jnp.where((named > 0.5) & (jnp.abs(rank - c) < 0.5), 1.0, 0.0)
        scale = jnp.sum(pick * weight, axis=1, keepdims=True)
        pick = pick.astype(BF)
        pick_ref[c * dests : (c + 1) * dests, :] = pick
        flat_ref[:, c * width : (c + 1) * width] = dot(pick, tok_ref[...])
        flat_ref[:, (CAP + c) * width : (CAP + c + 1) * width] = dot(pick, cot_ref[...]) * scale
    fold(lambda q: flat_ref[:, q * LANES : (q + 1) * LANES], fold_ref, home_ref)
    order = jnp.where(matched == across, 1.0, 0.0).astype(BF)
    flat_ref[...] = dot(order, flat_ref[...].astype(BF))
    fold(lambda q: flat_ref[:, q * LANES : (q + 1) * LANES], fold_ref, away_ref)


def pack(tokens, cotangent, routes, probs, matching):
    dests = matching.shape[0]
    rows, width = tokens.shape
    lanes = 2 * CAP * width
    buffer = jax.ShapeDtypeStruct((dests, lanes // LANES, LANES), BF)
    return pl.pallas_call(
        pack_kernel,
        out_shape=(buffer, buffer, jax.ShapeDtypeStruct((CAP * dests, rows), BF)),
        in_specs=[pl.BlockSpec(memory_space=pltpu.HBM)] * 5,
        out_specs=tuple(vmem(3)),
        scratch_shapes=[
            pltpu.VMEM(tokens.shape, BF),
            pltpu.VMEM(tokens.shape, BF),
            pltpu.VMEM(routes.shape[::-1], jnp.int32),
            pltpu.VMEM(routes.shape[::-1], F32),
            pltpu.VMEM((1, dests), jnp.int32),
            pltpu.VMEM((dests, lanes), F32),
            pltpu.VMEM((dests * lanes // LANES, LANES), F32),
            pltpu.SemaphoreType.DMA((5,)),
        ],
        compiler_params=params(whole=True),
    )(tokens, cotangent, routes.T, probs.T, matching.reshape(1, dests))


def stack_slots(block, first, width):
    return jnp.concatenate(
        [block[:, (first + c) * width : (first + c + 1) * width] for c in range(CAP)], axis=0
    )


def expert_kernel(rows_ref, gate_ref, up_ref, down_ref, parts_ref, factor_ref, fold_ref):
    slices, sources, _ = rows_ref.shape
    width = rows_ref.shape[2] // (2 * CAP)
    lanes = gate_ref.shape[2]

    def both(z):
        part = slice(z * width, (z + 1) * width)
        return jnp.concatenate([gate_ref[0, part, :], up_ref[0, part, :]], axis=1)

    two = jnp.zeros((CAP * sources, 2 * lanes), F32)
    hidden_back = jnp.zeros((CAP * sources, lanes), F32)
    for z in range(slices):
        block = rows_ref[z]
        two = two + dot(stack_slots(block, 0, width), both(z))
        hidden_back = hidden_back + dot(
            stack_slots(block, CAP, width), down_ref[0, z * width : (z + 1) * width, :]
        )
    gate, upper = two[:, :lanes], two[:, lanes:]
    sig = jax.nn.sigmoid(gate)
    hidden = (gate * sig * upper).astype(BF)
    up_back = (hidden_back * gate * sig).astype(BF)
    gate_back = (hidden_back * upper * sig * (1.0 + gate * (1.0 - sig))).astype(BF)
    pair = jnp.concatenate([gate_back, up_back], axis=1)
    for z in range(slices):
        parts_ref[z] = dot(pair, both(z), contract_cols).astype(BF)
    three = [v.astype(F32) for v in (gate_back, up_back, hidden)]
    blank = jnp.zeros((sources, LANES), F32)

    def block(q):
        c, k = divmod(q, 3)
        return three[k][c * sources : (c + 1) * sources, :] if c < CAP else blank

    fold(block, fold_ref, factor_ref)


def expert(rows, w_gate, w_up, w_down):
    slices, sources, lanes = rows.shape
    blocks = -(-CAP * 3 // 16) * 16
    return pl.pallas_call(
        expert_kernel,
        out_shape=(
            jax.ShapeDtypeStruct((slices, CAP * sources, lanes // (2 * CAP)), BF),
            jax.ShapeDtypeStruct((sources, blocks, LANES), BF),
        ),
        in_specs=vmem(4),
        out_specs=tuple(vmem(2)),
        scratch_shapes=[pltpu.VMEM((sources * blocks, LANES), F32)],
        compiler_params=params(),
    )(rows, w_gate, w_up, w_down)


def turn_kernel(offsets, me_ref, *refs):
    rows_hbm, (tokens_ref, grads_ref, rows_ref, sems) = refs[:-4], refs[-4:]
    width = rows_ref.shape[2] // (2 * CAP)
    copies = [
        pltpu.make_async_copy(r, rows_ref.at[i], sems.at[i]) for i, r in enumerate(rows_hbm)
    ]
    for c in copies:
        c.start()
    for i, c in enumerate(copies):
        c.wait()
        block = rows_ref[i]
        owner = lax.rem(me_ref[0] + (len(offsets) + offsets[i]), len(offsets))
        part = pl.ds(pl.multiple_of(owner * width, width), width)
        tokens_ref[part, :] = stack_slots(block, 0, width).T
        grads_ref[part, :] = stack_slots(block, CAP, width).T


def turn(me, offsets, rows):
    count = len(rows)
    sources, lanes = rows[0].shape
    out = jax.ShapeDtypeStruct((count * lanes // (2 * CAP), CAP * sources), BF)
    return pl.pallas_call(
        functools.partial(turn_kernel, offsets),
        out_shape=(out, out),
        in_specs=[pl.BlockSpec(memory_space=pltpu.SMEM)]
        + [pl.BlockSpec(memory_space=pltpu.HBM)] * count,
        out_specs=tuple(vmem(2)),
        scratch_shapes=[
            pltpu.VMEM((count, sources, lanes), BF),
            pltpu.SemaphoreType.DMA((count,)),
        ],
        compiler_params=params(),
        cost_estimate=pl.CostEstimate(
            flops=0, bytes_accessed=4 * count * sources * lanes, transcendentals=0
        ),
    )(me, *rows)


def outer_kernel(
    tokens_ref, grads_ref, moved_ref, gate_ref, up_ref, down_ref, wide_ref, factor_ref
):
    sources = moved_ref.shape[0]
    per = moved_ref.shape[1]
    lanes = gate_ref.shape[2]
    used = 3 * lanes // LANES

    @pl.when(pl.program_id(0) == 0)
    def _():
        wide_ref[...] = moved_ref[...].reshape(wide_ref.shape).astype(F32)
        for c in range(CAP):
            for k in range(used):
                block = wide_ref[pl.ds(c * used + k, sources, stride=per), :]
                factor_ref[c * sources : (c + 1) * sources, k * LANES : (k + 1) * LANES] = (
                    block.astype(BF)
                )

    two = dot(tokens_ref[...], factor_ref[:, : 2 * lanes])
    gate_ref[0] = two[:, :lanes]
    up_ref[0] = two[:, lanes:]
    down_ref[0] = dot(grads_ref[...], factor_ref[:, 2 * lanes :])


def outer(tokens, grads, moved, units):
    model, rows = tokens.shape
    steps = 4
    part = model // steps
    out = jax.ShapeDtypeStruct((1, model, units), F32)
    return pl.pallas_call(
        outer_kernel,
        grid=(steps,),
        out_shape=(out,) * 3,
        in_specs=[
            pl.BlockSpec((part, rows), lambda i: (i, 0)),
            pl.BlockSpec((part, rows), lambda i: (i, 0)),
            pl.BlockSpec(moved.shape, lambda i: (0, 0, 0)),
        ],
        out_specs=(pl.BlockSpec((1, part, units), lambda i: (0, i, 0)),) * 3,
        scratch_shapes=[
            pltpu.VMEM((moved.shape[0] * moved.shape[1], LANES), F32),
            pltpu.VMEM((rows, 3 * units), BF),
        ],
        compiler_params=params(),
        cost_estimate=pl.CostEstimate(
            flops=6 * rows * model * units,
            bytes_accessed=4 * tokens.size + 12 * model * units,
            transcendentals=0,
        ),
    )(tokens, grads, moved)


def relay_kernel(match_ref, src_ref, out_ref):
    for d in range(out_ref.shape[0]):
        out_ref[d] = src_ref[match_ref[d]]


def relay(blocks, matching):
    return pl.pallas_call(
        relay_kernel,
        out_shape=jax.ShapeDtypeStruct(blocks.shape, BF),
        in_specs=[pl.BlockSpec(memory_space=pltpu.SMEM)] + vmem(1),
        out_specs=pl.BlockSpec(memory_space=pltpu.VMEM),
        compiler_params=params(),
    )(matching, blocks)


def slots_kernel(rows_ref, out_ref):
    sources, width = out_ref.shape[0], rows_ref.shape[1]
    for c in range(CAP):
        out_ref[:, c * width : (c + 1) * width] = rows_ref[c * sources : (c + 1) * sources, :]


def slots_to_lanes(rows):
    count, width = rows.shape
    return pl.pallas_call(
        slots_kernel,
        out_shape=jax.ShapeDtypeStruct((count // CAP, CAP * width), BF),
        in_specs=vmem(1),
        out_specs=pl.BlockSpec(memory_space=pltpu.VMEM),
        compiler_params=params(),
    )(rows)


def combine_kernel(back_ref, pick_ref, out_ref):
    rows = stack_slots(back_ref[...], 0, out_ref.shape[1])
    out_ref[...] = dot(pick_ref[...], rows, contract_rows).astype(BF)


def combine(back, pick, shape):
    return pl.pallas_call(
        combine_kernel,
        out_shape=jax.ShapeDtypeStruct(shape, BF),
        in_specs=vmem(2),
        out_specs=pl.BlockSpec(memory_space=pltpu.VMEM),
        compiler_params=params(),
    )(back, pick)


def swap(x, axes):
    return lax.all_to_all(x, axes, split_axis=0, concat_axis=0, tiled=True)


def arrive(send):
    return swap(send, "expert").reshape(send.shape[0], send.shape[1] * LANES)


def around(x, step):
    count = lax.axis_size("dp")
    return lax.ppermute(x, "dp", [(i, (i + step) % count) for i in range(count)])


def collect(x):
    count = lax.axis_size("dp")
    found, offsets = [x], [0]
    right = left = x
    for k in range(1, count // 2 + 1):
        right = around(right, 1)
        found.append(right)
        offsets.append(-k)
        if k < count // 2:
            left = around(left, -1)
            found.append(left)
            offsets.append(k)
    return offsets, found


def local(tokens, cotangent, routes, probs, matching, gate_weight, up_weight, down_weight):
    experts = matching.shape[0]
    units = gate_weight.shape[2]
    width = tokens.shape[1]
    home, away, pick = pack(tokens, cotangent, routes, probs, matching)
    home_rows = lax.all_gather(arrive(home)[None], "dp", axis=0, tiled=True)
    home_rows, arrived = lax.optimization_barrier((home_rows, arrive(away)))
    offsets, away_rows = collect(arrived)
    parts, factors = expert(home_rows, gate_weight, up_weight, down_weight)
    pair_back = lax.psum_scatter(
        parts.reshape(-1, width), "dp", scatter_dimension=0, tiled=True
    )
    moved = swap(relay(swap(factors, "expert"), matching), "expert")
    pair_back, moved = lax.optimization_barrier((pair_back, moved))
    lanes = CAP * width
    back = swap(slots_to_lanes(pair_back).reshape(experts, 2, lanes // 2), "expert")
    turned, grads_turned = turn(lax.axis_index("dp").reshape(1), offsets, away_rows)
    gate_sum, up_sum, down_sum = outer(turned, grads_turned, moved, units)
    total = combine(back.reshape(experts, lanes), pick, tokens.shape)
    return (total, gate_sum, up_sum, down_sum)


def solution(mesh):
    placed = (
        P("expert", "dp"),
        P("expert", "dp"),
        P("expert", None),
        P("expert", None),
        P(),
        P("expert", None, "dp"),
        P("expert", None, "dp"),
        P("expert", None, "dp"),
    )
    return jax.shard_map(
        local,
        mesh=mesh,
        in_specs=placed,
        out_specs=(
            P("expert", "dp"),
            P("expert", None, "dp"),
            P("expert", None, "dp"),
            P("expert", None, "dp"),
        ),
        check_vma=False,
    )
```

time: 177 us -> 171 us (0.966)
  blocking collectives: 100 us -> 47 us
  starting transfers between devices: 9.97 us -> 52.2 us
  waiting for transfers between devices: 31.8 us -> 40 us
  local copies, waits for them, and re-layouts: 7.51 us -> 4.38 us
    all_to_all x3 -> x2, blocking collectives: 100 us -> 47 us  [swap(): return lax.all_to_all(x, axes, split_axis=0, concat_axis=0, tiled=True)]
    ppermute x0 -> x7, starting transfers between devices: none -> 21.4 us  [around(): lax.ppermute(x, 'dp', [(i, (i + step) % count) for i in range(count)])]
    all_to_all x2 -> x3, starting transfers between devices: 9.89 us -> 30.7 us  [swap(): return lax.all_to_all(x, axes, split_axis=0, concat_axis=0, tiled=True)]
    ppermute x0 -> x7, waiting for transfers between devices: none -> 6.39 us  [around(): lax.ppermute(x, 'dp', [(i, (i + step) % count) for i in range(count)])]
    reshape x4 -> x1, local copies, waits for them, and re-layouts: 3.28 us -> 0.71 us  [local(): slots_to_lanes(pair_back).reshape(experts, 2, lanes // 2)]
    all_gather x2 -> x1, waiting for transfers between devices: 20.8 us -> 22 us  [local(): home_rows = lax.all_gather(arrive(home)[None], 'dp', axis=0, tiled=True)]
    all_to_all x2 -> x3, waiting for transfers between devices: 11 us -> 11.6 us  [swap(): return lax.all_to_all(x, axes, split_axis=0, concat_axis=0, tiled=True)]
    pallas_call x5 -> x6, Pallas kernels: 10.2 us -> 9.87 us  [the longest x1 3.15 us: outer(): pl.pallas_call(outer_kernel, grid=(steps,), out_shape=(out,) * 3, in_spec...]
  transfers between devices with their start and end apart: 4 -> 12, of which waited for: 2 -> 4; matrix products, arithmetic and copies ran while one was open for 2% -> 0% of each run, Pallas kernels for 5% -> 4%
where the time goes in v4:
time: 171 us; the launch traced here: 170 us
  starting transfers between devices  52.2 us (31%)
  blocking collectives  47 us (27%)
  waiting for transfers between devices  40 us (23%)
  between operations  14.3 us (8%)
  Pallas kernels  12.1 us (7%)
  local copies, waits for them, and re-layouts  4.38 us (3%)
    all_to_all x2, blocking collectives, swap(): return lax.all_to_all(x, axes, split_axis=0, concat_axis=0, tiled=True)  47 us
    all_to_all x3, starting transfers between devices, swap(): return lax.all_to_all(x, axes, split_axis=0, concat_axis=0, tiled=True)  30.7 us
    all_gather x1, waiting for transfers between devices, local(): home_rows = lax.all_gather(arrive(home)[None], 'dp', axis=0, tiled=True)  22 us
    ppermute x7, starting transfers between devices, around(): lax.ppermute(x, 'dp', [(i, (i + step) % count) for i in range(count)])  21.4 us
    all_to_all x3, waiting for transfers between devices, swap(): return lax.all_to_all(x, axes, split_axis=0, concat_axis=0, tiled=True)  11.6 us
    ppermute x7, waiting for transfers between devices, around(): lax.ppermute(x, 'dp', [(i, (i + step) % count) for i in range(count)])  6.39 us
  transfers between devices with their start and end apart: 12, of which 4 were waited for; matrix products, arithmetic and copies ran while one was open for 0% of the time, Pallas kernels for 4%

profile of v4, /device:TPU:1, one launch (start us, length us, event | category | flops | bytes accessed | tf_op | source)
XLA Modules:
  0.0 170.0 jit_solution(8600523962549804733)
XLA Ops:
  7.2 0.0 all-gather.2.cloned.1.call-start
  7.2 2.2 %shard_map.111 = (bf16[64,20,128]{2,1,0:T(8,128)(2,1)}, bf16[64,20,128]{2,1,0:T(8,128)(2,1)}, bf16[320,32]{1,0:T(8,128)(2,1)}) custom-call(bf16[32,256]{1,0:T(8,128)(2,1)} %tok_hbm.1, bf16[32,256]{1,0:T(8,128)(2,1)} %cot_hbm.1, s32[8,32]{1,0:T(8,128)} %bitcast.18, f32[8,32]{1,0:T(8,128)} %bitcast.19, s32[1,64]{1,0:T(1,128)} %bitcast.15), custom_call_target="tpu_custom_call" | custom-call | tf_op jit(solution)/shard_map/pallas_call | solution.py:91
  9.5 0.0 copy-start.7
  9.5 0.0 copy-start.1
  9.5 0.0 copy-start.2
  9.5 0.0 copy-start.3
  9.5 26.4 %all_to_all.25 = bf16[64,20,128]{2,1,0:T(8,128)(2,1)S(1)} all-to-all(bf16[64,20,128]{2,1,0:T(8,128)(2,1)} %get-tuple-element.18), channel_id=1, replica_groups=mesh['dp'=8,'expert'=64] {'expert'}, dimensions={0} | all-to-all | bytes 655360 | tf_op jit(solution)/shard_map/all_to_all | solution.py:305
  35.9 0.9 broadcast_in_dim_reshape.3
  36.8 0.0 all-gather.2.cloned.1.call-update
  36.8 0.0 reduce-scatter.2.cloned.1.call-start
  36.9 0.0 copy-done.7
  36.9 20.6 %all_to_all.26 = bf16[64,20,128]{2,1,0:T(8,128)(2,1)S(1)} all-to-all(bf16[64,20,128]{2,1,0:T(8,128)(2,1)S(1)} %copy-done.7), channel_id=1, replica_groups=mesh['dp'=8,'expert'=64] {'expert'}, dimensions={0} | all-to-all | bytes 655360 | tf_op jit(solution)/shard_map/all_to_all | solution.py:305
  57.6 22.0 %all-gather.2.cloned.1.call-done.rows_ref = bf16[8,64,2560]{2,1,0:T(8,128)(2,1)} async-done(((bf16[1,64,2560]{2,1,0:T(8,128)(2,1)}), bf16[8,64,2560]{2,1,0:T(8,128)(2,1)}) %all-gather.2.cloned.1.call-update) | async-done | bytes 2621456 | tf_op jit(solution)/shard_map/all_gather | solution.py:337
  79.6 0.0 copy-done.1
  79.6 0.0 copy-done.2
  79.6 0.0 copy-done.3
  79.6 1.7 %copy-done = bf16[8,64,2560]{2,1,0:T(8,128)(2,1)S(1)} copy-done((bf16[8,64,2560]{2,1,0:T(8,128)(2,1)S(1)}, bf16[8,64,2560]{2,1,0:T(8,128)(2,1)}, u32[]{:S(2)}) %copy-start) | copy-done | bytes 2621464
  81.3 2.5 %shard_map.112 = (bf16[8,320,256]{2,1,0:T(8,128)(2,1)}, bf16[64,16,128]{2,1,0:T(8,128)(2,1)}) custom-call(bf16[8,64,2560]{2,1,0:T(8,128)(2,1)S(1)} %copy-done, bf16[1,2048,128]{2,1,0:T(8,128)(2,1)S(1)} %copy-done.1, bf16[1,2048,128]{2,1,0:T(8,128)(2,1)S(1)} %copy-done.2, bf16[1,2048,128]{2,1,0:T(8,128)(2,1)S(1)} %copy-done.3), custom_call_target="tpu_custom_call" | custom-call | tf_op jit(solution)/shard_map/pallas_call | solution.py:154
  83.8 0.0 reduce-scatter.2.cloned.1.call-update
  83.8 3.1 %collective-permute-start = (bf16[64,2560]{1,0:T(8,128)(2,1)S(1)}, bf16[64,2560]{1,0:T(8,128)(2,1)S(1)}, u32[]{:S(2)}, u32[]{:S(2)}) collective-permute-start(bf16[64,2560]{1,0:T(8,128)(2,1)S(1)} %bitcast.11), channel_id=1, source_target_pairs={{0,64},{64,128},{128,192},{192,256},{256,320},{320,384},{384,448},... | collective-permute-start | bytes 983048 | tf_op jit(solution)/shard_map/ppermute | solution.py:314
  86.9 13.6 %all-to-all-start.2 = ((bf16[64,16,128]{2,1,0:T(8,128)(2,1)}), bf16[64,16,128]{2,1,0:T(8,128)(2,1)S(1)}, u32[]{:S(2)}, u32[]{:S(2)}) async-start(bf16[64,16,128]{2,1,0:T(8,128)(2,1)} %get-tuple-element.22), calls=%async_computation.3 | async-start | bytes 524288 | tf_op jit(solution)/shard_map/all_to_all | solution.py:305
  100.5 3.7 %collective-permute-start.1 = (bf16[64,2560]{1,0:T(8,128)(2,1)S(1)}, bf16[64,2560]{1,0:T(8,128)(2,1)S(1)}, u32[]{:S(2)}, u32[]{:S(2)}) collective-permute-start(bf16[64,2560]{1,0:T(8,128)(2,1)S(1)} %bitcast.12), channel_id=1, source_target_pairs={{0,448},{64,0},{128,64},{192,128},{256,192},{320,256},{384,320},{4... | collective-permute-start | bytes 983048 | tf_op jit(solution)/shard_map/ppermute | solution.py:314
  104.2 0.0 collective-permute-done.refs_1_
  104.2 1.9 %collective-permute-start.2 = (bf16[64,2560]{1,0:T(8,128)(2,1)S(1)}, bf16[64,2560]{1,0:T(8,128)(2,1)S(1)}, u32[]{:S(2)}, u32[]{:S(2)}) collective-permute-start(bf16[64,2560]{1,0:T(8,128)(2,1)S(1)} %collective-permute-done.refs_1_), channel_id=1, source_target_pairs={{0,64},{64,128},{128,192},{192,256},{256,320},{320,384},{384,448},... | collective-permute-start | bytes 983048 | tf_op jit(solution)/shard_map/ppermute | solution.py:314
  106.2 6.3 %all-to-all-done.2.src_ref = bf16[64,16,128]{2,1,0:T(8,128)(2,1)S(1)} async-done(((bf16[64,16,128]{2,1,0:T(8,128)(2,1)}), bf16[64,16,128]{2,1,0:T(8,128)(2,1)S(1)}, u32[]{:S(2)}, u32[]{:S(2)}) %all-to-all-start.2) | async-done | bytes 262176 | tf_op jit(solution)/shard_map/all_to_all | solution.py:305
  112.5 0.0 copy-done.6
  112.5 1.3 shard_map.113
  113.8 6.0 %all-to-all-start.3 = ((bf16[64,16,128]{2,1,0:T(8,128)(2,1)}), bf16[64,16,128]{2,1,0:T(8,128)(2,1)S(1)}, u32[]{:S(2)}, u32[]{:S(2)}) async-start(bf16[64,16,128]{2,1,0:T(8,128)(2,1)} %shard_map.113), calls=%async_computation.4 | async-start | bytes 524288 | tf_op jit(solution)/shard_map/all_to_all | solution.py:305
  119.8 0.0 collective-permute-done.1.refs_2_
  119.8 3.7 %collective-permute-start.3 = (bf16[64,2560]{1,0:T(8,128)(2,1)S(1)}, bf16[64,2560]{1,0:T(8,128)(2,1)S(1)}, u32[]{:S(2)}, u32[]{:S(2)}) collective-permute-start(bf16[64,2560]{1,0:T(8,128)(2,1)S(1)} %collective-permute-done.1.refs_2_), channel_id=1, source_target_pairs={{0,448},{64,0},{128,64},{192,128},{256,192},{320,256},{384,320},{4... | collective-permute-start | bytes 983048 | tf_op jit(solution)/shard_map/ppermute | solution.py:314
  123.6 0.0 collective-permute-done.2.refs_3_
  123.6 1.9 %collective-permute-start.4 = (bf16[64,2560]{1,0:T(8,128)(2,1)S(1)}, bf16[64,2560]{1,0:T(8,128)(2,1)S(1)}, u32[]{:S(2)}, u32[]{:S(2)}) collective-permute-start(bf16[64,2560]{1,0:T(8,128)(2,1)S(1)} %collective-permute-done.2.refs_3_), channel_id=1, source_target_pairs={{0,64},{64,128},{128,192},{192,256},{256,320},{320,384},{384,448},... | collective-permute-start | bytes 983048 | tf_op jit(solution)/shard_map/ppermute | solution.py:314
  125.5 6.4 %collective-permute-done.3.refs_4_ = bf16[64,2560]{1,0:T(8,128)(2,1)S(1)} collective-permute-done((bf16[64,2560]{1,0:T(8,128)(2,1)S(1)}, bf16[64,2560]{1,0:T(8,128)(2,1)S(1)}, u32[]{:S(2)}, u32[]{:S(2)}) %collective-permute-start.3) | collective-permute-done | bytes 327712 | tf_op jit(solution)/shard_map/ppermute | solution.py:314
  131.9 5.1 %collective-permute-start.5 = (bf16[64,2560]{1,0:T(8,128)(2,1)S(1)}, bf16[64,2560]{1,0:T(8,128)(2,1)S(1)}, u32[]{:S(2)}, u32[]{:S(2)}) collective-permute-start(bf16[64,2560]{1,0:T(8,128)(2,1)S(1)} %collective-permute-done.3.refs_4_), channel_id=1, source_target_pairs={{0,448},{64,0},{128,64},{192,128},{256,192},{320,256},{384,320},{4... | collective-permute-start | bytes 983048 | tf_op jit(solution)/shard_map/ppermute | solution.py:314
  137.0 0.0 collective-permute-done.4.refs_5_
  137.0 1.9 %collective-permute-start.6 = (bf16[64,2560]{1,0:T(8,128)(2,1)S(1)}, bf16[64,2560]{1,0:T(8,128)(2,1)S(1)}, u32[]{:S(2)}, u32[]{:S(2)}) collective-permute-start(bf16[64,2560]{1,0:T(8,128)(2,1)S(1)} %collective-permute-done.4.refs_5_), channel_id=1, source_target_pairs={{0,64},{64,128},{128,192},{192,256},{256,320},{320,384},{384,448},... | collective-permute-start | bytes 983048 | tf_op jit(solution)/shard_map/ppermute | solution.py:314
  139.0 0.0 all-to-all-done.3.moved_ref
  139.0 0.0 reduce-scatter.2.cloned.1.call-done.rows_ref
  139.0 0.9 copy-done.4
  139.9 0.7 reshape.29
  140.6 11.1 %all-to-all-start.4 = ((bf16[64,2,640]{2,1,0:T(2,128)(2,1)}), bf16[64,2,640]{2,1,0:T(2,128)(2,1)S(1)}, u32[]{:S(2)}, u32[]{:S(2)}) async-start(bf16[64,2,640]{2,1,0:T(2,128)(2,1)} %reshape.29), calls=%async_computation.5 | async-start | bytes 327680 | tf_op jit(solution)/shard_map/all_to_all | solution.py:305
  151.8 0.0 collective-permute-done.5.refs_6_
  151.8 0.0 collective-permute-done.6.refs_7_
  151.8 2.2 %shard_map.116 = (bf16[2048,320]{1,0:T(8,128)(2,1)S(1)}, bf16[2048,320]{1,0:T(8,128)(2,1)S(1)}) custom-call(s32[1]{0:T(128)} %bitcast.4.me_ref, bf16[64,2560]{1,0:T(8,128)(2,1)S(1)} %bitcast.13, bf16[64,2560]{1,0:T(8,128)(2,1)S(1)} %collective-permute-done.refs_1_, bf16[64,2560]{1,0:T(8,128)(2,1)S(1)} %collective-permute-done.1.refs_2_, ...), custom_call_target="tpu_custom_call" | custom-call | bytes 5242880 | tf_op jit(solution)/shard_map/pallas_call | solution.py:188
  154.0 3.2 %shard_map.117 = (f32[1,2048,128]{2,1,0:T(8,128)}, f32[1,2048,128]{2,1,0:T(8,128)}, f32[1,2048,128]{2,1,0:T(8,128)}) custom-call(bf16[2048,320]{1,0:T(8,128)(2,1)S(1)} %get-tuple-element.26.tokens_ref, bf16[2048,320]{1,0:T(8,128)(2,1)S(1)} %get-tuple-element.27.grads_ref, bf16[64,16,128]{2,1,0:T(8,128)(2,1)S(1)} %all-to-all-done.3.moved_ref), custom_call_target="tpu_custom_call" | custom-call | flops 503316480 | bytes 5767168 | tf_op jit(solution)/shard_map/pallas_call | solution.py:234
  157.1 5.2 %all-to-all-done.4 = bf16[64,2,640]{2,1,0:T(2,128)(2,1)S(1)} async-done(((bf16[64,2,640]{2,1,0:T(2,128)(2,1)}), bf16[64,2,640]{2,1,0:T(2,128)(2,1)S(1)}, u32[]{:S(2)}, u32[]{:S(2)}) %all-to-all-start.4) | async-done | bytes 163872 | tf_op jit(solution)/shard_map/all_to_all | solution.py:305
  162.4 0.0 copy-done.5
  162.4 0.8 shard_map.115
  (7 shorter events, 0.1 us)
Async XLA Ops:
  7.2 72.4 %all-gather.2.cloned.1.call-start = ((), (), s32[]{:S(2)}) async-start(), calls=%async_computation.6 | async-start | bytes 2949120 | tf_op jit(solution)/shard_map/all_gather | solution.py:337
  9.5 27.4 %copy-start.7 = (bf16[64,20,128]{2,1,0:T(8,128)(2,1)S(1)}, bf16[64,20,128]{2,1,0:T(8,128)(2,1)}, u32[]{:S(2)}) copy-start(bf16[64,20,128]{2,1,0:T(8,128)(2,1)} %get-tuple-element.19) | copy-start | bytes 983044
  9.5 70.1 %copy-start.1 = (bf16[1,2048,128]{2,1,0:T(8,128)(2,1)S(1)}, bf16[1,2048,128]{2,1,0:T(8,128)(2,1)}, u32[]{:S(2)}) copy-start(bf16[1,2048,128]{2,1,0:T(8,128)(2,1)} %gate_ref.1) | copy-start | bytes 1572868
  9.5 70.1 %copy-start.2 = (bf16[1,2048,128]{2,1,0:T(8,128)(2,1)S(1)}, bf16[1,2048,128]{2,1,0:T(8,128)(2,1)}, u32[]{:S(2)}) copy-start(bf16[1,2048,128]{2,1,0:T(8,128)(2,1)} %up_ref.1) | copy-start | bytes 1572868
  9.5 70.1 %copy-start.3 = (bf16[1,2048,128]{2,1,0:T(8,128)(2,1)S(1)}, bf16[1,2048,128]{2,1,0:T(8,128)(2,1)}, u32[]{:S(2)}) copy-start(bf16[1,2048,128]{2,1,0:T(8,128)(2,1)} %down_ref.1) | copy-start | bytes 1572868
  36.8 102.2 %reduce-scatter.2.cloned.1.call-start = ((), (), s32[]{:S(2)}) async-start(), calls=%async_computation.7 | async-start | bytes 1474560 | tf_op jit(solution)/shard_map/reduce_scatter | solution.py:341
  79.6 1.7 %copy-start = (bf16[8,64,2560]{2,1,0:T(8,128)(2,1)S(1)}, bf16[8,64,2560]{2,1,0:T(8,128)(2,1)}, u32[]{:S(2)}) copy-start(bf16[8,64,2560]{2,1,0:T(8,128)(2,1)} %all-gather.2.cloned.1.call-done.rows_ref) | copy-start | bytes 7864324
  83.8 28.7 %copy-start.6 = (s32[64]{0:T(128)S(1)}, s32[64]{0:T(128)}, u32[]{:S(2)}) copy-start(s32[64]{0:T(128)} %match_ref.1) | copy-start | bytes 772
  83.8 20.4 %collective-permute-start = (bf16[64,2560]{1,0:T(8,128)(2,1)S(1)}, bf16[64,2560]{1,0:T(8,128)(2,1)S(1)}, u32[]{:S(2)}, u32[]{:S(2)}) collective-permute-start(bf16[64,2560]{1,0:T(8,128)(2,1)S(1)} %bitcast.11), channel_id=1, source_target_pairs={{0,64},{64,128},{128,192},{192,256},{256,320},{320,384},{384,448},... | collective-permute-start | bytes 983048 | tf_op jit(solution)/shard_map/ppermute | solution.py:314
  86.9 25.6 %all-to-all-start.2 = ((bf16[64,16,128]{2,1,0:T(8,128)(2,1)}), bf16[64,16,128]{2,1,0:T(8,128)(2,1)S(1)}, u32[]{:S(2)}, u32[]{:S(2)}) async-start(bf16[64,16,128]{2,1,0:T(8,128)(2,1)} %get-tuple-element.22), calls=%async_computation.3 | async-start | bytes 524288 | tf_op jit(solution)/shard_map/all_to_all | solution.py:305
  100.5 19.3 %collective-permute-start.1 = (bf16[64,2560]{1,0:T(8,128)(2,1)S(1)}, bf16[64,2560]{1,0:T(8,128)(2,1)S(1)}, u32[]{:S(2)}, u32[]{:S(2)}) collective-permute-start(bf16[64,2560]{1,0:T(8,128)(2,1)S(1)} %bitcast.12), channel_id=1, source_target_pairs={{0,448},{64,0},{128,64},{192,128},{256,192},{320,256},{384,320},{4... | collective-permute-start | bytes 983048 | tf_op jit(solution)/shard_map/ppermute | solution.py:314
  104.2 19.3 %collective-permute-start.2 = (bf16[64,2560]{1,0:T(8,128)(2,1)S(1)}, bf16[64,2560]{1,0:T(8,128)(2,1)S(1)}, u32[]{:S(2)}, u32[]{:S(2)}) collective-permute-start(bf16[64,2560]{1,0:T(8,128)(2,1)S(1)} %collective-permute-done.refs_1_), channel_id=1, source_target_pairs={{0,64},{64,128},{128,192},{192,256},{256,320},{320,384},{384,448},... | collective-permute-start | bytes 983048 | tf_op jit(solution)/shard_map/ppermute | solution.py:314
  113.8 25.2 %all-to-all-start.3 = ((bf16[64,16,128]{2,1,0:T(8,128)(2,1)}), bf16[64,16,128]{2,1,0:T(8,128)(2,1)S(1)}, u32[]{:S(2)}, u32[]{:S(2)}) async-start(bf16[64,16,128]{2,1,0:T(8,128)(2,1)} %shard_map.113), calls=%async_computation.4 | async-start | bytes 524288 | tf_op jit(solution)/shard_map/all_to_all | solution.py:305
  119.8 12.0 %collective-permute-start.3 = (bf16[64,2560]{1,0:T(8,128)(2,1)S(1)}, bf16[64,2560]{1,0:T(8,128)(2,1)S(1)}, u32[]{:S(2)}, u32[]{:S(2)}) collective-permute-start(bf16[64,2560]{1,0:T(8,128)(2,1)S(1)} %collective-permute-done.1.refs_2_), channel_id=1, source_target_pairs={{0,448},{64,0},{128,64},{192,128},{256,192},{320,256},{384,320},{4... | collective-permute-start | bytes 983048 | tf_op jit(solution)/shard_map/ppermute | solution.py:314
  123.6 13.5 %collective-permute-start.4 = (bf16[64,2560]{1,0:T(8,128)(2,1)S(1)}, bf16[64,2560]{1,0:T(8,128)(2,1)S(1)}, u32[]{:S(2)}, u32[]{:S(2)}) collective-permute-start(bf16[64,2560]{1,0:T(8,128)(2,1)S(1)} %collective-permute-done.2.refs_3_), channel_id=1, source_target_pairs={{0,64},{64,128},{128,192},{192,256},{256,320},{320,384},{384,448},... | collective-permute-start | bytes 983048 | tf_op jit(solution)/shard_map/ppermute | solution.py:314
  131.9 19.9 %collective-permute-start.5 = (bf16[64,2560]{1,0:T(8,128)(2,1)S(1)}, bf16[64,2560]{1,0:T(8,128)(2,1)S(1)}, u32[]{:S(2)}, u32[]{:S(2)}) collective-permute-start(bf16[64,2560]{1,0:T(8,128)(2,1)S(1)} %collective-permute-done.3.refs_4_), channel_id=1, source_target_pairs={{0,448},{64,0},{128,64},{192,128},{256,192},{320,256},{384,320},{4... | collective-permute-start | bytes 983048 | tf_op jit(solution)/shard_map/ppermute | solution.py:314
  137.0 14.7 %collective-permute-start.6 = (bf16[64,2560]{1,0:T(8,128)(2,1)S(1)}, bf16[64,2560]{1,0:T(8,128)(2,1)S(1)}, u32[]{:S(2)}, u32[]{:S(2)}) collective-permute-start(bf16[64,2560]{1,0:T(8,128)(2,1)S(1)} %collective-permute-done.4.refs_5_), channel_id=1, source_target_pairs={{0,64},{64,128},{128,192},{192,256},{256,320},{320,384},{384,448},... | collective-permute-start | bytes 983048 | tf_op jit(solution)/shard_map/ppermute | solution.py:314
  139.0 0.9 copy-start.4
  140.6 21.7 %all-to-all-start.4 = ((bf16[64,2,640]{2,1,0:T(2,128)(2,1)}), bf16[64,2,640]{2,1,0:T(2,128)(2,1)S(1)}, u32[]{:S(2)}, u32[]{:S(2)}) async-start(bf16[64,2,640]{2,1,0:T(2,128)(2,1)} %reshape.29), calls=%async_computation.5 | async-start | bytes 327680 | tf_op jit(solution)/shard_map/all_to_all | solution.py:305
  153.9 8.4 %copy-start.5 = (bf16[320,32]{1,0:T(8,128)(2,1)S(1)}, bf16[320,32]{1,0:T(8,128)(2,1)}, u32[]{:S(2)}) copy-start(bf16[320,32]{1,0:T(8,128)(2,1)} %get-tuple-element.24.pick_ref) | copy-start | bytes 61444
Sparse Core Ops, SparseCore 0:
  37.0 42.5 all-gather.1
  83.9 42.3 reduce-scatter.1

commit v5 on v4

--- a/solution.py
+++ b/solution.py
@@ -33,7 +33,7 @@
     count, rows, _ = out_ref.shape
     for q in range(rows):
         scratch[pl.ds(q, count, stride=rows), :] = block(q)
-    out_ref[...] = scratch[...].reshape(out_ref.shape).astype(BF)
+    out_ref[...] = scratch[: count * rows, :].reshape(out_ref.shape).astype(BF)
 
 
 def pack_kernel(
@@ -100,7 +100,7 @@
             pltpu.VMEM(routes.shape[::-1], F32),
             pltpu.VMEM((1, dests), jnp.int32),
             pltpu.VMEM((dests, lanes), F32),
-            pltpu.VMEM((dests * lanes // LANES, LANES), F32),
+            pltpu.VMEM(((dests + 1) * lanes // LANES, LANES), F32),
             pltpu.SemaphoreType.DMA((5,)),
         ],
         compiler_params=params(whole=True),
@@ -159,7 +159,7 @@
         ),
         in_specs=vmem(4),
         out_specs=tuple(vmem(2)),
-        scratch_shapes=[pltpu.VMEM((sources * blocks, LANES), F32)],
+        scratch_shapes=[pltpu.VMEM(((sources + 1) * blocks, LANES), F32)],
         compiler_params=params(),
     )(rows, w_gate, w_up, w_down)
 
@@ -212,7 +212,7 @@
 
     @pl.when(pl.program_id(0) == 0)
     def _():
-        wide_ref[...] = moved_ref[...].reshape(wide_ref.shape).astype(F32)
+        wide_ref[: sources * per, :] = moved_ref[...].reshape(sources * per, LANES).astype(F32)
         for c in range(CAP):
             for k in range(used):
                 block = wide_ref[pl.ds(c * used + k, sources, stride=per), :]
@@ -242,7 +242,7 @@
         ],
         out_specs=(pl.BlockSpec((1, part, units), lambda i: (0, i, 0)),) * 3,
         scratch_shapes=[
-            pltpu.VMEM((moved.shape[0] * moved.shape[1], LANES), F32),
+            pltpu.VMEM(((moved.shape[0] + 1) * moved.shape[1], LANES), F32),
             pltpu.VMEM((rows, 3 * units), BF),
         ],
         compiler_params=params(),

time: 171 us -> 171 us (level)
  no operation moved by 1% of the time
where the time goes in v5:
time: 171 us; the launch traced here: 170 us
  starting transfers between devices  52.2 us (31%)
  blocking collectives  47 us (27%)
  waiting for transfers between devices  40 us (23%)
  between operations  14.3 us (8%)
  Pallas kernels  12.1 us (7%)
  local copies, waits for them, and re-layouts  4.38 us (3%)
    all_to_all x2, blocking collectives, swap(): return lax.all_to_all(x, axes, split_axis=0, concat_axis=0, tiled=True)  47 us
    all_to_all x3, starting transfers between devices, swap(): return lax.all_to_all(x, axes, split_axis=0, concat_axis=0, tiled=True)  30.6 us
    all_gather x1, waiting for transfers between devices, local(): home_rows = lax.all_gather(arrive(home)[None], 'dp', axis=0, tiled=True)  22 us
    ppermute x7, starting transfers between devices, around(): lax.ppermute(x, 'dp', [(i, (i + step) % count) for i in range(count)])  21.6 us
    all_to_all x3, waiting for transfers between devices, swap(): return lax.all_to_all(x, axes, split_axis=0, concat_axis=0, tiled=True)  11.6 us
    ppermute x7, waiting for transfers between devices, around(): lax.ppermute(x, 'dp', [(i, (i + step) % count) for i in range(count)])  6.39 us
  transfers between devices with their start and end apart: 12, of which 4 were waited for; matrix products, arithmetic and copies ran while one was open for 0% of the time, Pallas kernels for 4%

profile of v5, /device:TPU:1, one launch (start us, length us, event | category | flops | bytes accessed | tf_op | source)
XLA Modules:
  0.0 170.0 jit_solution(1447844573508870304)
XLA Ops:
  7.2 0.0 all-gather.2.cloned.1.call-start
  7.2 2.2 %shard_map.111 = (bf16[64,20,128]{2,1,0:T(8,128)(2,1)}, bf16[64,20,128]{2,1,0:T(8,128)(2,1)}, bf16[320,32]{1,0:T(8,128)(2,1)}) custom-call(bf16[32,256]{1,0:T(8,128)(2,1)} %tok_hbm.1, bf16[32,256]{1,0:T(8,128)(2,1)} %cot_hbm.1, s32[8,32]{1,0:T(8,128)} %bitcast.18, f32[8,32]{1,0:T(8,128)} %bitcast.19, s32[1,64]{1,0:T(1,128)} %bitcast.15), custom_call_target="tpu_custom_call" | custom-call | tf_op jit(solution)/shard_map/pallas_call | solution.py:91
  9.5 0.0 copy-start.7
  9.5 0.0 copy-start.1
  9.5 0.0 copy-start.2
  9.5 0.0 copy-start.3
  9.5 26.4 %all_to_all.25 = bf16[64,20,128]{2,1,0:T(8,128)(2,1)S(1)} all-to-all(bf16[64,20,128]{2,1,0:T(8,128)(2,1)} %get-tuple-element.18), channel_id=1, replica_groups=mesh['dp'=8,'expert'=64] {'expert'}, dimensions={0} | all-to-all | bytes 655360 | tf_op jit(solution)/shard_map/all_to_all | solution.py:305
  35.9 0.9 broadcast_in_dim_reshape.3
  36.8 0.0 all-gather.2.cloned.1.call-update
  36.8 0.0 reduce-scatter.2.cloned.1.call-start
  36.9 0.0 copy-done.7
  36.9 20.6 %all_to_all.26 = bf16[64,20,128]{2,1,0:T(8,128)(2,1)S(1)} all-to-all(bf16[64,20,128]{2,1,0:T(8,128)(2,1)S(1)} %copy-done.7), channel_id=1, replica_groups=mesh['dp'=8,'expert'=64] {'expert'}, dimensions={0} | all-to-all | bytes 655360 | tf_op jit(solution)/shard_map/all_to_all | solution.py:305
  57.6 22.0 %all-gather.2.cloned.1.call-done.rows_ref = bf16[8,64,2560]{2,1,0:T(8,128)(2,1)} async-done(((bf16[1,64,2560]{2,1,0:T(8,128)(2,1)}), bf16[8,64,2560]{2,1,0:T(8,128)(2,1)}) %all-gather.2.cloned.1.call-update) | async-done | bytes 2621456 | tf_op jit(solution)/shard_map/all_gather | solution.py:337
  79.6 0.0 copy-done.1
  79.6 0.0 copy-done.2
  79.6 0.0 copy-done.3
  79.6 1.7 %copy-done = bf16[8,64,2560]{2,1,0:T(8,128)(2,1)S(1)} copy-done((bf16[8,64,2560]{2,1,0:T(8,128)(2,1)S(1)}, bf16[8,64,2560]{2,1,0:T(8,128)(2,1)}, u32[]{:S(2)}) %copy-start) | copy-done | bytes 2621464
  81.3 2.5 %shard_map.112 = (bf16[8,320,256]{2,1,0:T(8,128)(2,1)}, bf16[64,16,128]{2,1,0:T(8,128)(2,1)}) custom-call(bf16[8,64,2560]{2,1,0:T(8,128)(2,1)S(1)} %copy-done, bf16[1,2048,128]{2,1,0:T(8,128)(2,1)S(1)} %copy-done.1, bf16[1,2048,128]{2,1,0:T(8,128)(2,1)S(1)} %copy-done.2, bf16[1,2048,128]{2,1,0:T(8,128)(2,1)S(1)} %copy-done.3), custom_call_target="tpu_custom_call" | custom-call | tf_op jit(solution)/shard_map/pallas_call | solution.py:154
  83.8 0.0 reduce-scatter.2.cloned.1.call-update
  83.8 3.1 %collective-permute-start = (bf16[64,2560]{1,0:T(8,128)(2,1)S(1)}, bf16[64,2560]{1,0:T(8,128)(2,1)S(1)}, u32[]{:S(2)}, u32[]{:S(2)}) collective-permute-start(bf16[64,2560]{1,0:T(8,128)(2,1)S(1)} %bitcast.11), channel_id=1, source_target_pairs={{0,64},{64,128},{128,192},{192,256},{256,320},{320,384},{384,448},... | collective-permute-start | bytes 983048 | tf_op jit(solution)/shard_map/ppermute | solution.py:314
  86.9 13.6 %all-to-all-start.2 = ((bf16[64,16,128]{2,1,0:T(8,128)(2,1)}), bf16[64,16,128]{2,1,0:T(8,128)(2,1)S(1)}, u32[]{:S(2)}, u32[]{:S(2)}) async-start(bf16[64,16,128]{2,1,0:T(8,128)(2,1)} %get-tuple-element.22), calls=%async_computation.3 | async-start | bytes 524288 | tf_op jit(solution)/shard_map/all_to_all | solution.py:305
  100.5 3.7 %collective-permute-start.1 = (bf16[64,2560]{1,0:T(8,128)(2,1)S(1)}, bf16[64,2560]{1,0:T(8,128)(2,1)S(1)}, u32[]{:S(2)}, u32[]{:S(2)}) collective-permute-start(bf16[64,2560]{1,0:T(8,128)(2,1)S(1)} %bitcast.12), channel_id=1, source_target_pairs={{0,448},{64,0},{128,64},{192,128},{256,192},{320,256},{384,320},{4... | collective-permute-start | bytes 983048 | tf_op jit(solution)/shard_map/ppermute | solution.py:314
  104.2 0.0 collective-permute-done.refs_1_
  104.2 1.9 %collective-permute-start.2 = (bf16[64,2560]{1,0:T(8,128)(2,1)S(1)}, bf16[64,2560]{1,0:T(8,128)(2,1)S(1)}, u32[]{:S(2)}, u32[]{:S(2)}) collective-permute-start(bf16[64,2560]{1,0:T(8,128)(2,1)S(1)} %collective-permute-done.refs_1_), channel_id=1, source_target_pairs={{0,64},{64,128},{128,192},{192,256},{256,320},{320,384},{384,448},... | collective-permute-start | bytes 983048 | tf_op jit(solution)/shard_map/ppermute | solution.py:314
  106.2 6.3 %all-to-all-done.2.src_ref = bf16[64,16,128]{2,1,0:T(8,128)(2,1)S(1)} async-done(((bf16[64,16,128]{2,1,0:T(8,128)(2,1)}), bf16[64,16,128]{2,1,0:T(8,128)(2,1)S(1)}, u32[]{:S(2)}, u32[]{:S(2)}) %all-to-all-start.2) | async-done | bytes 262176 | tf_op jit(solution)/shard_map/all_to_all | solution.py:305
  112.5 0.0 copy-done.6
  112.5 1.3 shard_map.113
  113.8 6.0 %all-to-all-start.3 = ((bf16[64,16,128]{2,1,0:T(8,128)(2,1)}), bf16[64,16,128]{2,1,0:T(8,128)(2,1)S(1)}, u32[]{:S(2)}, u32[]{:S(2)}) async-start(bf16[64,16,128]{2,1,0:T(8,128)(2,1)} %shard_map.113), calls=%async_computation.4 | async-start | bytes 524288 | tf_op jit(solution)/shard_map/all_to_all | solution.py:305
  119.8 0.0 collective-permute-done.1.refs_2_
  119.8 3.7 %collective-permute-start.3 = (bf16[64,2560]{1,0:T(8,128)(2,1)S(1)}, bf16[64,2560]{1,0:T(8,128)(2,1)S(1)}, u32[]{:S(2)}, u32[]{:S(2)}) collective-permute-start(bf16[64,2560]{1,0:T(8,128)(2,1)S(1)} %collective-permute-done.1.refs_2_), channel_id=1, source_target_pairs={{0,448},{64,0},{128,64},{192,128},{256,192},{320,256},{384,320},{4... | collective-permute-start | bytes 983048 | tf_op jit(solution)/shard_map/ppermute | solution.py:314
  123.6 0.0 collective-permute-done.2.refs_3_
  123.6 1.9 %collective-permute-start.4 = (bf16[64,2560]{1,0:T(8,128)(2,1)S(1)}, bf16[64,2560]{1,0:T(8,128)(2,1)S(1)}, u32[]{:S(2)}, u32[]{:S(2)}) collective-permute-start(bf16[64,2560]{1,0:T(8,128)(2,1)S(1)} %collective-permute-done.2.refs_3_), channel_id=1, source_target_pairs={{0,64},{64,128},{128,192},{192,256},{256,320},{320,384},{384,448},... | collective-permute-start | bytes 983048 | tf_op jit(solution)/shard_map/ppermute | solution.py:314
  125.5 6.4 %collective-permute-done.3.refs_4_ = bf16[64,2560]{1,0:T(8,128)(2,1)S(1)} collective-permute-done((bf16[64,2560]{1,0:T(8,128)(2,1)S(1)}, bf16[64,2560]{1,0:T(8,128)(2,1)S(1)}, u32[]{:S(2)}, u32[]{:S(2)}) %collective-permute-start.3) | collective-permute-done | bytes 327712 | tf_op jit(solution)/shard_map/ppermute | solution.py:314
  131.9 5.3 %collective-permute-start.5 = (bf16[64,2560]{1,0:T(8,128)(2,1)S(1)}, bf16[64,2560]{1,0:T(8,128)(2,1)S(1)}, u32[]{:S(2)}, u32[]{:S(2)}) collective-permute-start(bf16[64,2560]{1,0:T(8,128)(2,1)S(1)} %collective-permute-done.3.refs_4_), channel_id=1, source_target_pairs={{0,448},{64,0},{128,64},{192,128},{256,192},{320,256},{384,320},{4... | collective-permute-start | bytes 983048 | tf_op jit(solution)/shard_map/ppermute | solution.py:314
  137.1 0.0 collective-permute-done.4.refs_5_
  137.2 1.9 %collective-permute-start.6 = (bf16[64,2560]{1,0:T(8,128)(2,1)S(1)}, bf16[64,2560]{1,0:T(8,128)(2,1)S(1)}, u32[]{:S(2)}, u32[]{:S(2)}) collective-permute-start(bf16[64,2560]{1,0:T(8,128)(2,1)S(1)} %collective-permute-done.4.refs_5_), channel_id=1, source_target_pairs={{0,64},{64,128},{128,192},{192,256},{256,320},{320,384},{384,448},... | collective-permute-start | bytes 983048 | tf_op jit(solution)/shard_map/ppermute | solution.py:314
  139.1 0.0 all-to-all-done.3.moved_ref
  139.1 0.0 reduce-scatter.2.cloned.1.call-done.rows_ref
  139.1 0.9 copy-done.4
  140.1 0.7 reshape.29
  140.8 11.0 %all-to-all-start.4 = ((bf16[64,2,640]{2,1,0:T(2,128)(2,1)}), bf16[64,2,640]{2,1,0:T(2,128)(2,1)S(1)}, u32[]{:S(2)}, u32[]{:S(2)}) async-start(bf16[64,2,640]{2,1,0:T(2,128)(2,1)} %reshape.29), calls=%async_computation.5 | async-start | bytes 327680 | tf_op jit(solution)/shard_map/all_to_all | solution.py:305
  151.8 0.0 collective-permute-done.5.refs_6_
  151.8 0.0 collective-permute-done.6.refs_7_
  151.8 2.2 %shard_map.116 = (bf16[2048,320]{1,0:T(8,128)(2,1)S(1)}, bf16[2048,320]{1,0:T(8,128)(2,1)S(1)}) custom-call(s32[1]{0:T(128)} %bitcast.4.me_ref, bf16[64,2560]{1,0:T(8,128)(2,1)S(1)} %bitcast.13, bf16[64,2560]{1,0:T(8,128)(2,1)S(1)} %collective-permute-done.refs_1_, bf16[64,2560]{1,0:T(8,128)(2,1)S(1)} %collective-permute-done.1.refs_2_, ...), custom_call_target="tpu_custom_call" | custom-call | bytes 5242880 | tf_op jit(solution)/shard_map/pallas_call | solution.py:188
  154.0 3.2 %shard_map.117 = (f32[1,2048,128]{2,1,0:T(8,128)}, f32[1,2048,128]{2,1,0:T(8,128)}, f32[1,2048,128]{2,1,0:T(8,128)}) custom-call(bf16[2048,320]{1,0:T(8,128)(2,1)S(1)} %get-tuple-element.26.tokens_ref, bf16[2048,320]{1,0:T(8,128)(2,1)S(1)} %get-tuple-element.27.grads_ref, bf16[64,16,128]{2,1,0:T(8,128)(2,1)S(1)} %all-to-all-done.3.moved_ref), custom_call_target="tpu_custom_call" | custom-call | flops 503316480 | bytes 5767168 | tf_op jit(solution)/shard_map/pallas_call | solution.py:234
  157.1 5.2 %all-to-all-done.4 = bf16[64,2,640]{2,1,0:T(2,128)(2,1)S(1)} async-done(((bf16[64,2,640]{2,1,0:T(2,128)(2,1)}), bf16[64,2,640]{2,1,0:T(2,128)(2,1)S(1)}, u32[]{:S(2)}, u32[]{:S(2)}) %all-to-all-start.4) | async-done | bytes 163872 | tf_op jit(solution)/shard_map/all_to_all | solution.py:305
  162.4 0.0 copy-done.5
  162.4 0.8 shard_map.115
  (7 shorter events, 0.1 us)
Async XLA Ops:
  7.2 72.4 %all-gather.2.cloned.1.call-start = ((), (), s32[]{:S(2)}) async-start(), calls=%async_computation.6 | async-start | bytes 2949120 | tf_op jit(solution)/shard_map/all_gather | solution.py:337
  9.5 27.4 %copy-start.7 = (bf16[64,20,128]{2,1,0:T(8,128)(2,1)S(1)}, bf16[64,20,128]{2,1,0:T(8,128)(2,1)}, u32[]{:S(2)}) copy-start(bf16[64,20,128]{2,1,0:T(8,128)(2,1)} %get-tuple-element.19) | copy-start | bytes 983044
  9.5 70.1 %copy-start.1 = (bf16[1,2048,128]{2,1,0:T(8,128)(2,1)S(1)}, bf16[1,2048,128]{2,1,0:T(8,128)(2,1)}, u32[]{:S(2)}) copy-start(bf16[1,2048,128]{2,1,0:T(8,128)(2,1)} %gate_ref.1) | copy-start | bytes 1572868
  9.5 70.1 %copy-start.2 = (bf16[1,2048,128]{2,1,0:T(8,128)(2,1)S(1)}, bf16[1,2048,128]{2,1,0:T(8,128)(2,1)}, u32[]{:S(2)}) copy-start(bf16[1,2048,128]{2,1,0:T(8,128)(2,1)} %up_ref.1) | copy-start | bytes 1572868
  9.5 70.1 %copy-start.3 = (bf16[1,2048,128]{2,1,0:T(8,128)(2,1)S(1)}, bf16[1,2048,128]{2,1,0:T(8,128)(2,1)}, u32[]{:S(2)}) copy-start(bf16[1,2048,128]{2,1,0:T(8,128)(2,1)} %down_ref.1) | copy-start | bytes 1572868
  36.8 102.3 %reduce-scatter.2.cloned.1.call-start = ((), (), s32[]{:S(2)}) async-start(), calls=%async_computation.7 | async-start | bytes 1474560 | tf_op jit(solution)/shard_map/reduce_scatter | solution.py:341
  79.6 1.7 %copy-start = (bf16[8,64,2560]{2,1,0:T(8,128)(2,1)S(1)}, bf16[8,64,2560]{2,1,0:T(8,128)(2,1)}, u32[]{:S(2)}) copy-start(bf16[8,64,2560]{2,1,0:T(8,128)(2,1)} %all-gather.2.cloned.1.call-done.rows_ref) | copy-start | bytes 7864324
  83.8 28.7 %copy-start.6 = (s32[64]{0:T(128)S(1)}, s32[64]{0:T(128)}, u32[]{:S(2)}) copy-start(s32[64]{0:T(128)} %match_ref.1) | copy-start | bytes 772
  83.8 20.4 %collective-permute-start = (bf16[64,2560]{1,0:T(8,128)(2,1)S(1)}, bf16[64,2560]{1,0:T(8,128)(2,1)S(1)}, u32[]{:S(2)}, u32[]{:S(2)}) collective-permute-start(bf16[64,2560]{1,0:T(8,128)(2,1)S(1)} %bitcast.11), channel_id=1, source_target_pairs={{0,64},{64,128},{128,192},{192,256},{256,320},{320,384},{384,448},... | collective-permute-start | bytes 983048 | tf_op jit(solution)/shard_map/ppermute | solution.py:314
  86.9 25.6 %all-to-all-start.2 = ((bf16[64,16,128]{2,1,0:T(8,128)(2,1)}), bf16[64,16,128]{2,1,0:T(8,128)(2,1)S(1)}, u32[]{:S(2)}, u32[]{:S(2)}) async-start(bf16[64,16,128]{2,1,0:T(8,128)(2,1)} %get-tuple-element.22), calls=%async_computation.3 | async-start | bytes 524288 | tf_op jit(solution)/shard_map/all_to_all | solution.py:305
  100.5 19.3 %collective-permute-start.1 = (bf16[64,2560]{1,0:T(8,128)(2,1)S(1)}, bf16[64,2560]{1,0:T(8,128)(2,1)S(1)}, u32[]{:S(2)}, u32[]{:S(2)}) collective-permute-start(bf16[64,2560]{1,0:T(8,128)(2,1)S(1)} %bitcast.12), channel_id=1, source_target_pairs={{0,448},{64,0},{128,64},{192,128},{256,192},{320,256},{384,320},{4... | collective-permute-start | bytes 983048 | tf_op jit(solution)/shard_map/ppermute | solution.py:314
  104.2 19.3 %collective-permute-start.2 = (bf16[64,2560]{1,0:T(8,128)(2,1)S(1)}, bf16[64,2560]{1,0:T(8,128)(2,1)S(1)}, u32[]{:S(2)}, u32[]{:S(2)}) collective-permute-start(bf16[64,2560]{1,0:T(8,128)(2,1)S(1)} %collective-permute-done.refs_1_), channel_id=1, source_target_pairs={{0,64},{64,128},{128,192},{192,256},{256,320},{320,384},{384,448},... | collective-permute-start | bytes 983048 | tf_op jit(solution)/shard_map/ppermute | solution.py:314
  113.8 25.3 %all-to-all-start.3 = ((bf16[64,16,128]{2,1,0:T(8,128)(2,1)}), bf16[64,16,128]{2,1,0:T(8,128)(2,1)S(1)}, u32[]{:S(2)}, u32[]{:S(2)}) async-start(bf16[64,16,128]{2,1,0:T(8,128)(2,1)} %shard_map.113), calls=%async_computation.4 | async-start | bytes 524288 | tf_op jit(solution)/shard_map/all_to_all | solution.py:305
  119.8 12.0 %collective-permute-start.3 = (bf16[64,2560]{1,0:T(8,128)(2,1)S(1)}, bf16[64,2560]{1,0:T(8,128)(2,1)S(1)}, u32[]{:S(2)}, u32[]{:S(2)}) collective-permute-start(bf16[64,2560]{1,0:T(8,128)(2,1)S(1)} %collective-permute-done.1.refs_2_), channel_id=1, source_target_pairs={{0,448},{64,0},{128,64},{192,128},{256,192},{320,256},{384,320},{4... | collective-permute-start | bytes 983048 | tf_op jit(solution)/shard_map/ppermute | solution.py:314
  123.6 13.6 %collective-permute-start.4 = (bf16[64,2560]{1,0:T(8,128)(2,1)S(1)}, bf16[64,2560]{1,0:T(8,128)(2,1)S(1)}, u32[]{:S(2)}, u32[]{:S(2)}) collective-permute-start(bf16[64,2560]{1,0:T(8,128)(2,1)S(1)} %collective-permute-done.2.refs_3_), channel_id=1, source_target_pairs={{0,64},{64,128},{128,192},{192,256},{256,320},{320,384},{384,448},... | collective-permute-start | bytes 983048 | tf_op jit(solution)/shard_map/ppermute | solution.py:314
  131.9 19.9 %collective-permute-start.5 = (bf16[64,2560]{1,0:T(8,128)(2,1)S(1)}, bf16[64,2560]{1,0:T(8,128)(2,1)S(1)}, u32[]{:S(2)}, u32[]{:S(2)}) collective-permute-start(bf16[64,2560]{1,0:T(8,128)(2,1)S(1)} %collective-permute-done.3.refs_4_), channel_id=1, source_target_pairs={{0,448},{64,0},{128,64},{192,128},{256,192},{320,256},{384,320},{4... | collective-permute-start | bytes 983048 | tf_op jit(solution)/shard_map/ppermute | solution.py:314
  137.2 14.6 %collective-permute-start.6 = (bf16[64,2560]{1,0:T(8,128)(2,1)S(1)}, bf16[64,2560]{1,0:T(8,128)(2,1)S(1)}, u32[]{:S(2)}, u32[]{:S(2)}) collective-permute-start(bf16[64,2560]{1,0:T(8,128)(2,1)S(1)} %collective-permute-done.4.refs_5_), channel_id=1, source_target_pairs={{0,64},{64,128},{128,192},{192,256},{256,320},{320,384},{384,448},... | collective-permute-start | bytes 983048 | tf_op jit(solution)/shard_map/ppermute | solution.py:314
  139.1 0.9 copy-start.4
  140.8 21.6 %all-to-all-start.4 = ((bf16[64,2,640]{2,1,0:T(2,128)(2,1)}), bf16[64,2,640]{2,1,0:T(2,128)(2,1)S(1)}, u32[]{:S(2)}, u32[]{:S(2)}) async-start(bf16[64,2,640]{2,1,0:T(2,128)(2,1)} %reshape.29), calls=%async_computation.5 | async-start | bytes 327680 | tf_op jit(solution)/shard_map/all_to_all | solution.py:305
  153.9 8.4 %copy-start.5 = (bf16[320,32]{1,0:T(8,128)(2,1)S(1)}, bf16[320,32]{1,0:T(8,128)(2,1)}, u32[]{:S(2)}) copy-start(bf16[320,32]{1,0:T(8,128)(2,1)} %get-tuple-element.24.pick_ref) | copy-start | bytes 61444
Sparse Core Ops, SparseCore 0:
  37.0 42.5 all-gather.1
  83.9 42.1 reduce-scatter.1

commit v6 on v5

--- a/solution.py
+++ b/solution.py
@@ -269,23 +269,6 @@
     )(matching, blocks)
 
 
-def slots_kernel(rows_ref, out_ref):
-    sources, width = out_ref.shape[0], rows_ref.shape[1]
-    for c in range(CAP):
-        out_ref[:, c * width : (c + 1) * width] = rows_ref[c * sources : (c + 1) * sources, :]
-
-
-def slots_to_lanes(rows):
-    count, width = rows.shape
-    return pl.pallas_call(
-        slots_kernel,
-        out_shape=jax.ShapeDtypeStruct((count // CAP, CAP * width), BF),
-        in_specs=vmem(1),
-        out_specs=pl.BlockSpec(memory_space=pltpu.VMEM),
-        compiler_params=params(),
-    )(rows)
-
-
 def combine_kernel(back_ref, pick_ref, out_ref):
     rows = stack_slots(back_ref[...], 0, out_ref.shape[1])
     out_ref[...] = dot(pick_ref[...], rows, contract_rows).astype(BF)
@@ -344,7 +327,8 @@
     moved = swap(relay(swap(factors, "expert"), matching), "expert")
     pair_back, moved = lax.optimization_barrier((pair_back, moved))
     lanes = CAP * width
-    back = swap(slots_to_lanes(pair_back).reshape(experts, 2, lanes // 2), "expert")
+    back = pair_back.reshape(CAP, experts, width).transpose(1, 0, 2)
+    back = swap(back.reshape(experts, 2, lanes // 2), "expert")
     turned, grads_turned = turn(lax.axis_index("dp").reshape(1), offsets, away_rows)
     gate_sum, up_sum, down_sum = outer(turned, grads_turned, moved, units)
     total = combine(back.reshape(experts, lanes), pick, tokens.shape)

time: 171 us -> 171 us (level)
  transfers between devices with their start and end apart: 12 -> 12, of which waited for: 4 -> 4; matrix products, arithmetic and copies ran while one was open for 0% -> 1% of each run, Pallas kernels for 4% -> 4%
where the time goes in v6:
time: 171 us; the launch traced here: 170 us
  starting transfers between devices  52.2 us (31%)
  blocking collectives  47 us (27%)
  waiting for transfers between devices  40.1 us (23%)
  between operations  14.3 us (8%)
  Pallas kernels  12.1 us (7%)
  local copies, waits for them, and re-layouts  4.58 us (3%)
    all_to_all x2, blocking collectives, swap(): return lax.all_to_all(x, axes, split_axis=0, concat_axis=0, tiled=True)  47 us
    all_to_all x3, starting transfers between devices, swap(): return lax.all_to_all(x, axes, split_axis=0, concat_axis=0, tiled=True)  30.7 us
    all_gather x1, waiting for transfers between devices, local(): home_rows = lax.all_gather(arrive(home)[None], 'dp', axis=0, tiled=True)  22 us
    ppermute x7, starting transfers between devices, around(): lax.ppermute(x, 'dp', [(i, (i + step) % count) for i in range(count)])  21.4 us
    all_to_all x3, waiting for transfers between devices, swap(): return lax.all_to_all(x, axes, split_axis=0, concat_axis=0, tiled=True)  11.6 us
    ppermute x7, waiting for transfers between devices, around(): lax.ppermute(x, 'dp', [(i, (i + step) % count) for i in range(count)])  6.46 us
  transfers between devices with their start and end apart: 12, of which 4 were waited for; matrix products, arithmetic and copies ran while one was open for 1% of the time, Pallas kernels for 4%

profile of v6, /device:TPU:1, one launch (start us, length us, event | category | flops | bytes accessed | tf_op | source)
XLA Modules:
  0.0 170.2 jit_solution(17148457975399062259)
XLA Ops:
  7.2 0.0 all-gather.2.cloned.1.call-start
  7.2 2.2 %shard_map.111 = (bf16[64,20,128]{2,1,0:T(8,128)(2,1)}, bf16[64,20,128]{2,1,0:T(8,128)(2,1)}, bf16[320,32]{1,0:T(8,128)(2,1)}) custom-call(bf16[32,256]{1,0:T(8,128)(2,1)} %tok_hbm.1, bf16[32,256]{1,0:T(8,128)(2,1)} %cot_hbm.1, s32[8,32]{1,0:T(8,128)} %bitcast.22, f32[8,32]{1,0:T(8,128)} %bitcast.23, s32[1,64]{1,0:T(1,128)} %bitcast.18), custom_call_target="tpu_custom_call" | custom-call | tf_op jit(solution)/shard_map/pallas_call | solution.py:91
  9.5 0.0 copy-start.6
  9.5 0.0 copy-start.1
  9.5 0.0 copy-start.2
  9.5 0.0 copy-start.3
  9.5 26.4 %all_to_all.25 = bf16[64,20,128]{2,1,0:T(8,128)(2,1)S(1)} all-to-all(bf16[64,20,128]{2,1,0:T(8,128)(2,1)} %get-tuple-element.18), channel_id=1, replica_groups=mesh['dp'=8,'expert'=64] {'expert'}, dimensions={0} | all-to-all | bytes 655360 | tf_op jit(solution)/shard_map/all_to_all | solution.py:288
  35.9 0.9 broadcast_in_dim_reshape.3
  36.8 0.0 all-gather.2.cloned.1.call-update
  36.8 0.0 reduce-scatter.2.cloned.1.call-start
  36.9 0.0 copy-done.6
  36.9 20.6 %all_to_all.26 = bf16[64,20,128]{2,1,0:T(8,128)(2,1)S(1)} all-to-all(bf16[64,20,128]{2,1,0:T(8,128)(2,1)S(1)} %copy-done.6), channel_id=1, replica_groups=mesh['dp'=8,'expert'=64] {'expert'}, dimensions={0} | all-to-all | bytes 655360 | tf_op jit(solution)/shard_map/all_to_all | solution.py:288
  57.6 22.0 %all-gather.2.cloned.1.call-done.rows_ref = bf16[8,64,2560]{2,1,0:T(8,128)(2,1)} async-done(((bf16[1,64,2560]{2,1,0:T(8,128)(2,1)}), bf16[8,64,2560]{2,1,0:T(8,128)(2,1)}) %all-gather.2.cloned.1.call-update) | async-done | bytes 2621456 | tf_op jit(solution)/shard_map/all_gather | solution.py:320
  79.6 0.0 copy-done.1
  79.6 0.0 copy-done.2
  79.6 0.0 copy-done.3
  79.6 1.7 %copy-done = bf16[8,64,2560]{2,1,0:T(8,128)(2,1)S(1)} copy-done((bf16[8,64,2560]{2,1,0:T(8,128)(2,1)S(1)}, bf16[8,64,2560]{2,1,0:T(8,128)(2,1)}, u32[]{:S(2)}) %copy-start) | copy-done | bytes 2621464
  81.3 2.4 %shard_map.112 = (bf16[8,320,256]{2,1,0:T(8,128)(2,1)}, bf16[64,16,128]{2,1,0:T(8,128)(2,1)}) custom-call(bf16[8,64,2560]{2,1,0:T(8,128)(2,1)S(1)} %copy-done, bf16[1,2048,128]{2,1,0:T(8,128)(2,1)S(1)} %copy-done.1, bf16[1,2048,128]{2,1,0:T(8,128)(2,1)S(1)} %copy-done.2, bf16[1,2048,128]{2,1,0:T(8,128)(2,1)S(1)} %copy-done.3), custom_call_target="tpu_custom_call" | custom-call | tf_op jit(solution)/shard_map/pallas_call | solution.py:154
  83.8 0.0 reduce-scatter.2.cloned.1.call-update
  83.8 3.1 %collective-permute-start = (bf16[64,2560]{1,0:T(8,128)(2,1)S(1)}, bf16[64,2560]{1,0:T(8,128)(2,1)S(1)}, u32[]{:S(2)}, u32[]{:S(2)}) collective-permute-start(bf16[64,2560]{1,0:T(8,128)(2,1)S(1)} %bitcast.14), channel_id=1, source_target_pairs={{0,64},{64,128},{128,192},{192,256},{256,320},{320,384},{384,448},... | collective-permute-start | bytes 983048 | tf_op jit(solution)/shard_map/ppermute | solution.py:297
  86.9 13.6 %all-to-all-start.2 = ((bf16[64,16,128]{2,1,0:T(8,128)(2,1)}), bf16[64,16,128]{2,1,0:T(8,128)(2,1)S(1)}, u32[]{:S(2)}, u32[]{:S(2)}) async-start(bf16[64,16,128]{2,1,0:T(8,128)(2,1)} %get-tuple-element.22), calls=%async_computation.3 | async-start | bytes 524288 | tf_op jit(solution)/shard_map/all_to_all | solution.py:288
  100.5 3.7 %collective-permute-start.1 = (bf16[64,2560]{1,0:T(8,128)(2,1)S(1)}, bf16[64,2560]{1,0:T(8,128)(2,1)S(1)}, u32[]{:S(2)}, u32[]{:S(2)}) collective-permute-start(bf16[64,2560]{1,0:T(8,128)(2,1)S(1)} %bitcast.15), channel_id=1, source_target_pairs={{0,448},{64,0},{128,64},{192,128},{256,192},{320,256},{384,320},{4... | collective-permute-start | bytes 983048 | tf_op jit(solution)/shard_map/ppermute | solution.py:297
  104.2 0.0 collective-permute-done.refs_1_
  104.2 1.9 %collective-permute-start.2 = (bf16[64,2560]{1,0:T(8,128)(2,1)S(1)}, bf16[64,2560]{1,0:T(8,128)(2,1)S(1)}, u32[]{:S(2)}, u32[]{:S(2)}) collective-permute-start(bf16[64,2560]{1,0:T(8,128)(2,1)S(1)} %collective-permute-done.refs_1_), channel_id=1, source_target_pairs={{0,64},{64,128},{128,192},{192,256},{256,320},{320,384},{384,448},... | collective-permute-start | bytes 983048 | tf_op jit(solution)/shard_map/ppermute | solution.py:297
  106.2 6.3 %all-to-all-done.2.src_ref = bf16[64,16,128]{2,1,0:T(8,128)(2,1)S(1)} async-done(((bf16[64,16,128]{2,1,0:T(8,128)(2,1)}), bf16[64,16,128]{2,1,0:T(8,128)(2,1)S(1)}, u32[]{:S(2)}, u32[]{:S(2)}) %all-to-all-start.2) | async-done | bytes 262176 | tf_op jit(solution)/shard_map/all_to_all | solution.py:288
  112.5 0.0 copy-done.5
  112.5 1.3 shard_map.113
  113.8 6.0 %all-to-all-start.3 = ((bf16[64,16,128]{2,1,0:T(8,128)(2,1)}), bf16[64,16,128]{2,1,0:T(8,128)(2,1)S(1)}, u32[]{:S(2)}, u32[]{:S(2)}) async-start(bf16[64,16,128]{2,1,0:T(8,128)(2,1)} %shard_map.113), calls=%async_computation.4 | async-start | bytes 524288 | tf_op jit(solution)/shard_map/all_to_all | solution.py:288
  119.8 0.0 collective-permute-done.1.refs_2_
  119.8 3.7 %collective-permute-start.3 = (bf16[64,2560]{1,0:T(8,128)(2,1)S(1)}, bf16[64,2560]{1,0:T(8,128)(2,1)S(1)}, u32[]{:S(2)}, u32[]{:S(2)}) collective-permute-start(bf16[64,2560]{1,0:T(8,128)(2,1)S(1)} %collective-permute-done.1.refs_2_), channel_id=1, source_target_pairs={{0,448},{64,0},{128,64},{192,128},{256,192},{320,256},{384,320},{4... | collective-permute-start | bytes 983048 | tf_op jit(solution)/shard_map/ppermute | solution.py:297
  123.6 0.0 collective-permute-done.2.refs_3_
  123.6 1.9 %collective-permute-start.4 = (bf16[64,2560]{1,0:T(8,128)(2,1)S(1)}, bf16[64,2560]{1,0:T(8,128)(2,1)S(1)}, u32[]{:S(2)}, u32[]{:S(2)}) collective-permute-start(bf16[64,2560]{1,0:T(8,128)(2,1)S(1)} %collective-permute-done.2.refs_3_), channel_id=1, source_target_pairs={{0,64},{64,128},{128,192},{192,256},{256,320},{320,384},{384,448},... | collective-permute-start | bytes 983048 | tf_op jit(solution)/shard_map/ppermute | solution.py:297
  125.5 6.4 %collective-permute-done.3.refs_4_ = bf16[64,2560]{1,0:T(8,128)(2,1)S(1)} collective-permute-done((bf16[64,2560]{1,0:T(8,128)(2,1)S(1)}, bf16[64,2560]{1,0:T(8,128)(2,1)S(1)}, u32[]{:S(2)}, u32[]{:S(2)}) %collective-permute-start.3) | collective-permute-done | bytes 327712 | tf_op jit(solution)/shard_map/ppermute | solution.py:297
  131.9 5.1 %collective-permute-start.5 = (bf16[64,2560]{1,0:T(8,128)(2,1)S(1)}, bf16[64,2560]{1,0:T(8,128)(2,1)S(1)}, u32[]{:S(2)}, u32[]{:S(2)}) collective-permute-start(bf16[64,2560]{1,0:T(8,128)(2,1)S(1)} %collective-permute-done.3.refs_4_), channel_id=1, source_target_pairs={{0,448},{64,0},{128,64},{192,128},{256,192},{320,256},{384,320},{4... | collective-permute-start | bytes 983048 | tf_op jit(solution)/shard_map/ppermute | solution.py:297
  137.1 0.0 collective-permute-done.4.refs_5_
  137.1 1.9 %collective-permute-start.6 = (bf16[64,2560]{1,0:T(8,128)(2,1)S(1)}, bf16[64,2560]{1,0:T(8,128)(2,1)S(1)}, u32[]{:S(2)}, u32[]{:S(2)}) collective-permute-start(bf16[64,2560]{1,0:T(8,128)(2,1)S(1)} %collective-permute-done.4.refs_5_), channel_id=1, source_target_pairs={{0,64},{64,128},{128,192},{192,256},{256,320},{320,384},{384,448},... | collective-permute-start | bytes 983048 | tf_op jit(solution)/shard_map/ppermute | solution.py:297
  139.0 0.0 all-to-all-done.3.moved_ref
  139.0 0.0 reduce-scatter.2.cloned.1.call-done
  139.1 1.0 copy.14
  140.1 0.8 reshape.33
  140.9 11.0 %all-to-all-start.4 = ((bf16[64,2,640]{2,1,0:T(2,128)(2,1)}), bf16[64,2,640]{2,1,0:T(2,128)(2,1)S(1)}, u32[]{:S(2)}, u32[]{:S(2)}) async-start(bf16[64,2,640]{2,1,0:T(2,128)(2,1)} %reshape.33), calls=%async_computation.5 | async-start | bytes 327680 | tf_op jit(solution)/shard_map/all_to_all | solution.py:288
  151.9 0.0 collective-permute-done.5.refs_6_
  151.9 0.0 collective-permute-done.6.refs_7_
  151.9 2.2 %shard_map.115 = (bf16[2048,320]{1,0:T(8,128)(2,1)S(1)}, bf16[2048,320]{1,0:T(8,128)(2,1)S(1)}) custom-call(s32[1]{0:T(128)} %bitcast.6.me_ref, bf16[64,2560]{1,0:T(8,128)(2,1)S(1)} %bitcast.16, bf16[64,2560]{1,0:T(8,128)(2,1)S(1)} %collective-permute-done.refs_1_, bf16[64,2560]{1,0:T(8,128)(2,1)S(1)} %collective-permute-done.1.refs_2_, ...), custom_call_target="tpu_custom_call" | custom-call | bytes 5242880 | tf_op jit(solution)/shard_map/pallas_call | solution.py:188
  154.1 0.0 copy-start.4
  154.1 3.2 %shard_map.116 = (f32[1,2048,128]{2,1,0:T(8,128)}, f32[1,2048,128]{2,1,0:T(8,128)}, f32[1,2048,128]{2,1,0:T(8,128)}) custom-call(bf16[2048,320]{1,0:T(8,128)(2,1)S(1)} %get-tuple-element.26.tokens_ref, bf16[2048,320]{1,0:T(8,128)(2,1)S(1)} %get-tuple-element.27.grads_ref, bf16[64,16,128]{2,1,0:T(8,128)(2,1)S(1)} %all-to-all-done.3.moved_ref), custom_call_target="tpu_custom_call" | custom-call | flops 503316480 | bytes 5767168 | tf_op jit(solution)/shard_map/pallas_call | solution.py:234
  157.3 5.2 %all-to-all-done.4 = bf16[64,2,640]{2,1,0:T(2,128)(2,1)S(1)} async-done(((bf16[64,2,640]{2,1,0:T(2,128)(2,1)}), bf16[64,2,640]{2,1,0:T(2,128)(2,1)S(1)}, u32[]{:S(2)}, u32[]{:S(2)}) %all-to-all-start.4) | async-done | bytes 163872 | tf_op jit(solution)/shard_map/all_to_all | solution.py:288
  162.5 0.8 shard_map.114
  (5 shorter events, 0.1 us)
Async XLA Ops:
  7.2 72.4 %all-gather.2.cloned.1.call-start = ((), (), s32[]{:S(2)}) async-start(), calls=%async_computation.6 | async-start | bytes 2949120 | tf_op jit(solution)/shard_map/all_gather | solution.py:320
  9.5 27.4 %copy-start.6 = (bf16[64,20,128]{2,1,0:T(8,128)(2,1)S(1)}, bf16[64,20,128]{2,1,0:T(8,128)(2,1)}, u32[]{:S(2)}) copy-start(bf16[64,20,128]{2,1,0:T(8,128)(2,1)} %get-tuple-element.19) | copy-start | bytes 983044
  9.5 70.1 %copy-start.1 = (bf16[1,2048,128]{2,1,0:T(8,128)(2,1)S(1)}, bf16[1,2048,128]{2,1,0:T(8,128)(2,1)}, u32[]{:S(2)}) copy-start(bf16[1,2048,128]{2,1,0:T(8,128)(2,1)} %gate_ref.1) | copy-start | bytes 1572868
  9.5 70.1 %copy-start.2 = (bf16[1,2048,128]{2,1,0:T(8,128)(2,1)S(1)}, bf16[1,2048,128]{2,1,0:T(8,128)(2,1)}, u32[]{:S(2)}) copy-start(bf16[1,2048,128]{2,1,0:T(8,128)(2,1)} %up_ref.1) | copy-start | bytes 1572868
  9.5 70.1 %copy-start.3 = (bf16[1,2048,128]{2,1,0:T(8,128)(2,1)S(1)}, bf16[1,2048,128]{2,1,0:T(8,128)(2,1)}, u32[]{:S(2)}) copy-start(bf16[1,2048,128]{2,1,0:T(8,128)(2,1)} %down_ref.1) | copy-start | bytes 1572868
  36.8 102.2 %reduce-scatter.2.cloned.1.call-start = ((), (), s32[]{:S(2)}) async-start(), calls=%async_computation.7 | async-start | bytes 1474560 | tf_op jit(solution)/shard_map/reduce_scatter | solution.py:324
  79.6 1.7 %copy-start = (bf16[8,64,2560]{2,1,0:T(8,128)(2,1)S(1)}, bf16[8,64,2560]{2,1,0:T(8,128)(2,1)}, u32[]{:S(2)}) copy-start(bf16[8,64,2560]{2,1,0:T(8,128)(2,1)} %all-gather.2.cloned.1.call-done.rows_ref) | copy-start | bytes 7864324
  83.8 28.7 %copy-start.5 = (s32[64]{0:T(128)S(1)}, s32[64]{0:T(128)}, u32[]{:S(2)}) copy-start(s32[64]{0:T(128)} %match_ref.1) | copy-start | bytes 772
  83.8 20.4 %collective-permute-start = (bf16[64,2560]{1,0:T(8,128)(2,1)S(1)}, bf16[64,2560]{1,0:T(8,128)(2,1)S(1)}, u32[]{:S(2)}, u32[]{:S(2)}) collective-permute-start(bf16[64,2560]{1,0:T(8,128)(2,1)S(1)} %bitcast.14), channel_id=1, source_target_pairs={{0,64},{64,128},{128,192},{192,256},{256,320},{320,384},{384,448},... | collective-permute-start | bytes 983048 | tf_op jit(solution)/shard_map/ppermute | solution.py:297
  86.9 25.6 %all-to-all-start.2 = ((bf16[64,16,128]{2,1,0:T(8,128)(2,1)}), bf16[64,16,128]{2,1,0:T(8,128)(2,1)S(1)}, u32[]{:S(2)}, u32[]{:S(2)}) async-start(bf16[64,16,128]{2,1,0:T(8,128)(2,1)} %get-tuple-element.22), calls=%async_computation.3 | async-start | bytes 524288 | tf_op jit(solution)/shard_map/all_to_all | solution.py:288
  100.5 19.3 %collective-permute-start.1 = (bf16[64,2560]{1,0:T(8,128)(2,1)S(1)}, bf16[64,2560]{1,0:T(8,128)(2,1)S(1)}, u32[]{:S(2)}, u32[]{:S(2)}) collective-permute-start(bf16[64,2560]{1,0:T(8,128)(2,1)S(1)} %bitcast.15), channel_id=1, source_target_pairs={{0,448},{64,0},{128,64},{192,128},{256,192},{320,256},{384,320},{4... | collective-permute-start | bytes 983048 | tf_op jit(solution)/shard_map/ppermute | solution.py:297
  104.2 19.3 %collective-permute-start.2 = (bf16[64,2560]{1,0:T(8,128)(2,1)S(1)}, bf16[64,2560]{1,0:T(8,128)(2,1)S(1)}, u32[]{:S(2)}, u32[]{:S(2)}) collective-permute-start(bf16[64,2560]{1,0:T(8,128)(2,1)S(1)} %collective-permute-done.refs_1_), channel_id=1, source_target_pairs={{0,64},{64,128},{128,192},{192,256},{256,320},{320,384},{384,448},... | collective-permute-start | bytes 983048 | tf_op jit(solution)/shard_map/ppermute | solution.py:297
  113.8 25.2 %all-to-all-start.3 = ((bf16[64,16,128]{2,1,0:T(8,128)(2,1)}), bf16[64,16,128]{2,1,0:T(8,128)(2,1)S(1)}, u32[]{:S(2)}, u32[]{:S(2)}) async-start(bf16[64,16,128]{2,1,0:T(8,128)(2,1)} %shard_map.113), calls=%async_computation.4 | async-start | bytes 524288 | tf_op jit(solution)/shard_map/all_to_all | solution.py:288
  119.8 12.1 %collective-permute-start.3 = (bf16[64,2560]{1,0:T(8,128)(2,1)S(1)}, bf16[64,2560]{1,0:T(8,128)(2,1)S(1)}, u32[]{:S(2)}, u32[]{:S(2)}) collective-permute-start(bf16[64,2560]{1,0:T(8,128)(2,1)S(1)} %collective-permute-done.1.refs_2_), channel_id=1, source_target_pairs={{0,448},{64,0},{128,64},{192,128},{256,192},{320,256},{384,320},{4... | collective-permute-start | bytes 983048 | tf_op jit(solution)/shard_map/ppermute | solution.py:297
  123.6 13.5 %collective-permute-start.4 = (bf16[64,2560]{1,0:T(8,128)(2,1)S(1)}, bf16[64,2560]{1,0:T(8,128)(2,1)S(1)}, u32[]{:S(2)}, u32[]{:S(2)}) collective-permute-start(bf16[64,2560]{1,0:T(8,128)(2,1)S(1)} %collective-permute-done.2.refs_3_), channel_id=1, source_target_pairs={{0,64},{64,128},{128,192},{192,256},{256,320},{320,384},{384,448},... | collective-permute-start | bytes 983048 | tf_op jit(solution)/shard_map/ppermute | solution.py:297
  131.9 20.0 %collective-permute-start.5 = (bf16[64,2560]{1,0:T(8,128)(2,1)S(1)}, bf16[64,2560]{1,0:T(8,128)(2,1)S(1)}, u32[]{:S(2)}, u32[]{:S(2)}) collective-permute-start(bf16[64,2560]{1,0:T(8,128)(2,1)S(1)} %collective-permute-done.3.refs_4_), channel_id=1, source_target_pairs={{0,448},{64,0},{128,64},{192,128},{256,192},{320,256},{384,320},{4... | collective-permute-start | bytes 983048 | tf_op jit(solution)/shard_map/ppermute | solution.py:297
  137.1 14.8 %collective-permute-start.6 = (bf16[64,2560]{1,0:T(8,128)(2,1)S(1)}, bf16[64,2560]{1,0:T(8,128)(2,1)S(1)}, u32[]{:S(2)}, u32[]{:S(2)}) collective-permute-start(bf16[64,2560]{1,0:T(8,128)(2,1)S(1)} %collective-permute-done.4.refs_5_), channel_id=1, source_target_pairs={{0,64},{64,128},{128,192},{192,256},{256,320},{320,384},{384,448},... | collective-permute-start | bytes 983048 | tf_op jit(solution)/shard_map/ppermute | solution.py:297
  140.9 21.6 %all-to-all-start.4 = ((bf16[64,2,640]{2,1,0:T(2,128)(2,1)}), bf16[64,2,640]{2,1,0:T(2,128)(2,1)S(1)}, u32[]{:S(2)}, u32[]{:S(2)}) async-start(bf16[64,2,640]{2,1,0:T(2,128)(2,1)} %reshape.33), calls=%async_computation.5 | async-start | bytes 327680 | tf_op jit(solution)/shard_map/all_to_all | solution.py:288
  154.1 8.4 %copy-start.4 = (bf16[320,32]{1,0:T(8,128)(2,1)S(1)}, bf16[320,32]{1,0:T(8,128)(2,1)}, u32[]{:S(2)}) copy-start(bf16[320,32]{1,0:T(8,128)(2,1)} %get-tuple-element.24.pick_ref) | copy-start | bytes 61444
Sparse Core Ops, SparseCore 0:
  37.0 42.5 all-gather.1
  83.9 42.5 reduce-scatter.1
